TPU v7x, 1024 devices: a whole 8x8x8 slice. The times are simulated.
1024 devices in a mesh: dp: 512 (over y_lo, x, z, core), sub: 2 (over y_hi).
Axes of the slice: x: 8, y: 8 (y_hi: 2, y_lo: 4; y = y_hi * 4 + y_lo), z: 8, core: 2. Of those that a mesh axis runs over, the one named last changes fastest.
Arguments:
- picture_encoder_embeds: float32 [131072, 1152], P(('dp', 'sub')), may hold values from -0.24 to 0.24
- caption_encoder_embeds: float32 [131072, 1152], P(('dp', 'sub')), may hold values from -0.24 to 0.24
- score_multiplier: float32 [], replicated, may hold values from 2 to 10
- score_offset_term: float32 [], replicated, may hold values from -4 to -1
Outputs:
- image_grad: float32 [131072, 1152], P(('dp', 'sub'))
- text_grad: float32 [131072, 1152], P(('dp', 'sub'))
All inputs are finite; a program needn't handle non-finite values.
Results may differ from a plain program's by a relative error of at most 0.005.
Values may be sent and summed in bfloat16 or wider, within the bound.
No kernel may reach another device: no remote copies, remote signals or barrier semaphores. Data moves between devices by JAX's collectives and lax.ppermute only.
A program may use at most 32 MiB of HBM per device.

v0:
```python
import jax
import jax.numpy as jnp
from jax import lax
from jax.sharding import PartitionSpec as P


def with_halo(block, sides, width):
    for axis, dim in sides:
        count = lax.axis_size(axis)
        forward = [(i, i + 1) for i in range(count - 1)]
        forward.append((count - 1, 0))
        backward = [(target, source) for source, target in forward]
        low = lax.ppermute(
            lax.slice_in_dim(block, block.shape[dim] - width, None, axis=dim), axis, forward
        )
        high = lax.ppermute(lax.slice_in_dim(block, 0, width, axis=dim), axis, backward)
        block = jnp.concatenate([low, block, high], axis=dim)
    return block


def from_behind(block, axis, distance):
    devices = range(lax.axis_size(axis))
    route = [((i - distance) % len(devices), i) for i in devices]
    return lax.ppermute(block, axis, route)


def normalize(values):
    inverse = lax.rsqrt(jnp.sum(values * values, axis=-1, keepdims=True) + 1e-06)
    return (values * inverse, inverse)


def backward_norm(unit, inverse, direction):
    return (direction - unit * jnp.sum(unit * direction, axis=-1, keepdims=True)) * inverse


def pair_coefficient_values(
    earlier_entries, later_entries, score_multiplier, score_offset_term, index_offset_amount
):
    similarity_scores = lax.dot_general(
        earlier_entries, later_entries, (((1,), (1,)), ((), ())), preferred_element_type=jnp.float32
    )
    similarity_scores = score_multiplier * similarity_scores + score_offset_term
    row_ids = lax.broadcasted_iota(jnp.int32, similarity_scores.shape, 0)
    col_ids = lax.broadcasted_iota(jnp.int32, similarity_scores.shape, 1)
    match_sign_label = jnp.where(
        col_ids == row_ids + index_offset_amount, jnp.float32(1.0), jnp.float32(-1.0)
    )
    return (
        -match_sign_label * score_multiplier * jax.nn.sigmoid(-match_sign_label * similarity_scores)
    ).astype(jnp.bfloat16)


def shards(picture_encoder_embeds, caption_encoder_embeds, score_multiplier, score_offset_term):
    image_unit, image_inverse = normalize(picture_encoder_embeds)
    text_unit, text_inverse = normalize(caption_encoder_embeds)
    picture_first_index = image_unit.astype(jnp.bfloat16)
    text_low = text_unit.astype(jnp.bfloat16)
    local_rows = picture_first_index.shape[0]
    partner_rows = lax.all_gather(text_low, "sub", axis=0, tiled=True)
    group_size = partner_rows.shape[0]
    nearby_strip_entries = with_halo(partner_rows, (("dp", 0),), group_size)
    index_offset_amount = lax.axis_index("sub") * local_rows + group_size
    derivative_weights = pair_coefficient_values(
        picture_first_index,
        nearby_strip_entries,
        score_multiplier,
        score_offset_term,
        index_offset_amount,
    )
    image_dir = jnp.dot(
        derivative_weights, nearby_strip_entries, preferred_element_type=jnp.float32
    )
    block_terms = jnp.einsum(
        "rc,rd->cd", derivative_weights, picture_first_index, preferred_element_type=jnp.float32
    )
    from_right = from_behind(block_terms[:group_size].astype(jnp.bfloat16), "dp", -1).astype(
        jnp.float32
    )
    from_left = from_behind(block_terms[2 * group_size :].astype(jnp.bfloat16), "dp", 1).astype(
        jnp.float32
    )
    group_terms = block_terms[group_size : 2 * group_size] + from_right + from_left
    text_dir = lax.psum_scatter(group_terms, "sub", scatter_dimension=0, tiled=True)
    image_grad = backward_norm(image_unit, image_inverse, image_dir)
    text_grad = backward_norm(text_unit, text_inverse, text_dir)
    return (image_grad, text_grad)


def solution(mesh):
    placed = (P(("dp", "sub"), None), P(("dp", "sub"), None), P(), P())
    return jax.shard_map(
        shards,
        mesh=mesh,
        in_specs=placed,
        out_specs=(P(("dp", "sub"), None), P(("dp", "sub"), None)),
        check_vma=False,
    )
```

profile of v0, /device:TPU:1, one launch (start us, length us, event | category | flops | bytes accessed | tf_op | source)
XLA Modules:
  0.0 139.7 jit_solution(6679309432022262400)
XLA Ops:
  7.2 0.0 copy-start
  7.2 0.0 reduce-scatter.2.cloned.1.call-start
  7.2 1.2 multiply_reduce_fusion.2
  8.5 1.2 multiply_convert_fusion
  9.6 11.7 %all_gather.3 = bf16[256,1152]{1,0:T(8,128)(2,1)S(1)} all-gather(bf16[128,1152]{1,0:T(8,128)(2,1)S(1)} %multiply_convert_fusion), channel_id=1, replica_groups=mesh['dp'=512,'sub'=2] {'sub'}, dimensions={0}, use_global_device_ids=true | all-gather | bytes 884736 | tf_op jit(solution)/shard_map/all_gather | solution.py:59
  21.4 10.1 %collective-permute-start = (bf16[256,1152]{1,0:T(8,128)(2,1)S(1)}, bf16[256,1152]{1,0:T(8,128)(2,1)}, u32[]{:S(2)}, u32[]{:S(2)}) collective-permute-start(bf16[256,1152]{1,0:T(8,128)(2,1)S(1)} %all_gather.3), channel_id=1, source_target_pairs={{0,2},{2,4},{4,6},{6,8},{8,10},{10,12},{12,14},{14,16},{16,18},{18... | collective-permute-start | bytes 1769480 | tf_op jit(solution)/shard_map/ppermute | solution.py:13
  31.5 7.4 %collective-permute-start.1 = (bf16[256,1152]{1,0:T(8,128)(2,1)S(1)}, bf16[256,1152]{1,0:T(8,128)(2,1)S(1)}, u32[]{:S(2)}, u32[]{:S(2)}) collective-permute-start(bf16[256,1152]{1,0:T(8,128)(2,1)S(1)} %all_gather.3), channel_id=1, source_target_pairs={{2,0},{4,2},{6,4},{8,6},{10,8},{12,10},{14,12},{16,14},{18,16},{20... | collective-permute-start | bytes 1769480 | tf_op jit(solution)/shard_map/ppermute | solution.py:16
  40.2 0.0 copy-done
  40.2 0.1 multiply_reduce_fusion.3
  40.4 0.0 collective-permute-done
  40.4 1.1 constant_dynamic-update-slice_fusion.2
  41.5 0.1 constant_dynamic-update-slice_fusion.1
  41.6 1.1 collective-permute-done.1
  42.7 0.1 constant_dynamic-update-slice_fusion
  42.8 0.7 fusion.8
  43.5 0.7 fusion.11
  44.2 0.1 fusion.10
  44.3 18.6 %collective-permute-start.2 = (bf16[256,1152]{1,0:T(8,128)(2,1)S(1)}, bf16[256,1152]{1,0:T(8,128)(2,1)S(1)}, u32[]{:S(2)}, u32[]{:S(2)}) collective-permute-start(bf16[256,1152]{1,0:T(8,128)(2,1)S(1)} %get-tuple-element.2), channel_id=1, source_target_pairs={{2,0},{4,2},{6,4},{8,6},{10,8},{12,10},{14,12},{16,14},{18,16},{20... | collective-permute-start | bytes 1769480 | tf_op jit(solution)/shard_map/ppermute | solution.py:24
  62.8 1.9 %collective-permute-start.3 = (bf16[256,1152]{1,0:T(8,128)(2,1)S(1)}, bf16[256,1152]{1,0:T(8,128)(2,1)S(1)}, u32[]{:S(2)}, u32[]{:S(2)}) collective-permute-start(bf16[256,1152]{1,0:T(8,128)(2,1)S(1)} %get-tuple-element.3), channel_id=1, source_target_pairs={{1022,0},{0,2},{2,4},{4,6},{6,8},{8,10},{10,12},{12,14},{14,16},{1... | collective-permute-start | bytes 1769480 | tf_op jit(solution)/shard_map/ppermute | solution.py:24
  64.8 0.0 collective-permute-done.2
  64.8 9.4 %collective-permute-done.3 = bf16[256,1152]{1,0:T(8,128)(2,1)S(1)} collective-permute-done((bf16[256,1152]{1,0:T(8,128)(2,1)S(1)}, bf16[256,1152]{1,0:T(8,128)(2,1)S(1)}, u32[]{:S(2)}, u32[]{:S(2)}) %collective-permute-start.3) | collective-permute-done | bytes 589856 | tf_op jit(solution)/shard_map/ppermute | solution.py:24
  74.2 1.2 fusion.7
  75.4 0.0 reduce-scatter.2.cloned.1.call-update
  75.4 0.0 copy-start.1
  75.4 0.5 multiply_reduce_fusion.1
  75.9 1.0 subtract_multiply_fusion.1
  76.9 52.7 %reduce-scatter.2.cloned.1.call-done = f32[128,1152]{1,0:T(8,128)} async-done(((f32[256,1152]{1,0:T(8,128)}), f32[128,1152]{1,0:T(8,128)}) %reduce-scatter.2.cloned.1.call-update) | async-done | bytes 589840 | tf_op jit(solution)/shard_map/reduce_scatter | solution.py:83
  129.6 0.0 copy-done.1
  129.6 1.3 multiply_reduce_fusion
  130.8 2.1 %subtract_multiply_fusion = f32[128,1152]{1,0:T(8,128)} fusion(f32[128,1152]{1,0:T(8,128)} %reduce-scatter.2.cloned.1.call-done, f32[128,1152]{1,0:T(8,128)S(1)} %copy-done.1, f32[128]{0:T(128)S(1)} %multiply_reduce_fusion, f32[128]{0:T(128)S(1)} %add_rsqrt_fusion), kind=kLoop, calls=%fused_computation.11 | loop fusion | flops 589824 | bytes 1770496 | tf_op jit(solution)/shard_map/mul | solution.py:33
  (3 shorter events, 0.0 us)
Async XLA Ops:
  7.2 33.1 %copy-start = (f32[128,1152]{1,0:T(8,128)S(1)}, f32[128,1152]{1,0:T(8,128)}, u32[]{:S(2)}) copy-start(f32[128,1152]{1,0:T(8,128)} %param.4) | copy-start | bytes 1769476
  7.2 122.4 %reduce-scatter.2.cloned.1.call-start = ((), (), s32[]{:S(2)}) async-start(), calls=%async_computation.1 | async-start | bytes 1769472 | tf_op jit(solution)/shard_map/reduce_scatter | solution.py:83
  21.4 19.0 %collective-permute-start = (bf16[256,1152]{1,0:T(8,128)(2,1)S(1)}, bf16[256,1152]{1,0:T(8,128)(2,1)}, u32[]{:S(2)}, u32[]{:S(2)}) collective-permute-start(bf16[256,1152]{1,0:T(8,128)(2,1)S(1)} %all_gather.3), channel_id=1, source_target_pairs={{0,2},{2,4},{4,6},{6,8},{8,10},{10,12},{12,14},{14,16},{16,18},{18... | collective-permute-start | bytes 1769480 | tf_op jit(solution)/shard_map/ppermute | solution.py:13
  31.5 11.2 %collective-permute-start.1 = (bf16[256,1152]{1,0:T(8,128)(2,1)S(1)}, bf16[256,1152]{1,0:T(8,128)(2,1)S(1)}, u32[]{:S(2)}, u32[]{:S(2)}) collective-permute-start(bf16[256,1152]{1,0:T(8,128)(2,1)S(1)} %all_gather.3), channel_id=1, source_target_pairs={{2,0},{4,2},{6,4},{8,6},{10,8},{12,10},{14,12},{16,14},{18,16},{20... | collective-permute-start | bytes 1769480 | tf_op jit(solution)/shard_map/ppermute | solution.py:16
  44.3 20.5 %collective-permute-start.2 = (bf16[256,1152]{1,0:T(8,128)(2,1)S(1)}, bf16[256,1152]{1,0:T(8,128)(2,1)S(1)}, u32[]{:S(2)}, u32[]{:S(2)}) collective-permute-start(bf16[256,1152]{1,0:T(8,128)(2,1)S(1)} %get-tuple-element.2), channel_id=1, source_target_pairs={{2,0},{4,2},{6,4},{8,6},{10,8},{12,10},{14,12},{16,14},{18,16},{20... | collective-permute-start | bytes 1769480 | tf_op jit(solution)/shard_map/ppermute | solution.py:24
  62.8 11.3 %collective-permute-start.3 = (bf16[256,1152]{1,0:T(8,128)(2,1)S(1)}, bf16[256,1152]{1,0:T(8,128)(2,1)S(1)}, u32[]{:S(2)}, u32[]{:S(2)}) collective-permute-start(bf16[256,1152]{1,0:T(8,128)(2,1)S(1)} %get-tuple-element.3), channel_id=1, source_target_pairs={{1022,0},{0,2},{2,4},{4,6},{6,8},{8,10},{10,12},{12,14},{14,16},{1... | collective-permute-start | bytes 1769480 | tf_op jit(solution)/shard_map/ppermute | solution.py:24
  75.4 54.2 %copy-start.1 = (f32[128,1152]{1,0:T(8,128)S(1)}, f32[128,1152]{1,0:T(8,128)}, u32[]{:S(2)}) copy-start(f32[128,1152]{1,0:T(8,128)} %param.5) | copy-start | bytes 1769476
Sparse Core Ops, SparseCore 0:
  75.5 54.0 reduce-scatter.1
where the time goes:
time: 140 us
  waiting for transfers between devices  63.2 us (45%)
  starting transfers between devices  38.1 us (27%)
  between operations  15.5 us (11%)
  blocking collectives  11.7 us (8%)
  other arithmetic  8.04 us (6%)
  matrix products  1.9 us (1%)
    reduce_scatter x1, waiting for transfers between devices, shards(): lax.psum_scatter(group_terms, 'sub', scatter_dimension=0, tiled=True)  52.7 us
    ppermute x2, starting transfers between devices, from_behind(): return lax.ppermute(block, axis, route)  20.5 us
    all_gather x1, blocking collectives, shards(): partner_rows = lax.all_gather(text_low, 'sub', axis=0, tiled=True)  11.7 us
    ppermute x1, starting transfers between devices, with_halo(): lax.ppermute(lax.slice_in_dim(block, block.shape[dim] - width, None, axis...  10.1 us
    ppermute x2, waiting for transfers between devices, from_behind(): return lax.ppermute(block, axis, route)  9.39 us
    ppermute x1, starting transfers between devices, with_halo(): lax.ppermute(lax.slice_in_dim(block, 0, width, axis=dim), axis, backward)  7.45 us
    mul x2, other arithmetic, backward_norm(): (direction - unit * jnp.sum(unit * direction, axis=-1, keepdims=True)) *...  3.04 us
  transfers between devices with their start and end apart: 5, of which 3 were waited for; matrix products, arithmetic and copies ran while one was open for 2% of the time, Pallas kernels for 0%

commit v1 on v0

v1 whole, which is shorter than its diff:
```python
import jax
import jax.numpy as jnp
from jax import lax
from jax.experimental import pallas as pl
from jax.experimental.pallas import tpu as pltpu
from jax.sharding import PartitionSpec as P

BF16 = jnp.bfloat16
F32 = jnp.float32
VMEM = pl.BlockSpec(memory_space=pltpu.VMEM)
SMEM = pl.BlockSpec(memory_space=pltpu.SMEM)


def times_transposed(a, b):
    return lax.dot_general(a, b, (((1,), (1,)), ((), ())), preferred_element_type=F32)


def times(a, b):
    return lax.dot_general(a, b, (((1,), (0,)), ((), ())), preferred_element_type=F32)


def inverse_norm(values):
    return lax.rsqrt(jnp.sum(values * values, axis=-1, keepdims=True) + 1e-06)


def backward_norm(values, direction):
    inverse = inverse_norm(values)
    unit = values * inverse
    return (direction - unit * jnp.sum(unit * direction, axis=-1, keepdims=True)) * inverse


def negative_coeffs(scale, offset, a, b):
    return (scale * jax.nn.sigmoid(scale * times_transposed(a, b) + offset)).astype(BF16)


def own_coeffs(scale, offset, a, b):
    scores = scale * times_transposed(a, b) + offset
    rows = lax.broadcasted_iota(jnp.int32, scores.shape, 0)
    columns = lax.broadcasted_iota(jnp.int32, scores.shape, 1)
    label = jnp.where(rows == columns, F32(1.0), F32(-1.0))
    return (-label * scale * jax.nn.sigmoid(-label * scores)).astype(BF16)


def normalize_kernel(values_ref, low_ref):
    values = values_ref[...]
    low_ref[...] = (values * inverse_norm(values)).astype(BF16)


def far_text_kernel(scale_ref, offset_ref, far_ref, own_ref, left_ref, right_ref, out_ref):
    scale, offset = scale_ref[0], offset_ref[0]
    far = far_ref[...]
    total = jnp.zeros(out_ref.shape, F32)
    for image_ref in (own_ref, left_ref, right_ref):
        image = image_ref[...]
        total += times(negative_coeffs(scale, offset, far, image), image)
    out_ref[...] = total.astype(BF16)


def near_kernel(
    scale_ref, offset_ref, image_ref, text_ref, left_image_ref, right_image_ref, left_text_ref, right_text_ref,
    image_dir_ref, text_dir_ref,
):
    scale, offset = scale_ref[0], offset_ref[0]
    image, text = image_ref[...], text_ref[...]
    image_dir = times(own_coeffs(scale, offset, image, text), text)
    text_dir = times(own_coeffs(scale, offset, text, image), image)
    for other_ref in (left_text_ref, right_text_ref):
        other = other_ref[...]
        image_dir += times(negative_coeffs(scale, offset, image, other), other)
    for other_ref in (left_image_ref, right_image_ref):
        other = other_ref[...]
        text_dir += times(negative_coeffs(scale, offset, text, other), other)
    image_dir_ref[...] = image_dir
    text_dir_ref[...] = text_dir


def image_kernel(
    scale_ref, offset_ref, image_ref, near_dir_ref, values_ref, far_ref, far_left_ref, far_right_ref, out_ref
):
    scale, offset = scale_ref[0], offset_ref[0]
    image = image_ref[...]
    direction = near_dir_ref[...]
    for text_ref in (far_ref, far_left_ref, far_right_ref):
        text = text_ref[...]
        direction += times(negative_coeffs(scale, offset, image, text), text)
    out_ref[...] = backward_norm(values_ref[...], direction)


def text_kernel(near_dir_ref, values_ref, far_dir_ref, out_ref):
    direction = near_dir_ref[...] + far_dir_ref[...].astype(F32)
    out_ref[...] = backward_norm(values_ref[...], direction)


def call(body, outs, operands, dots):
    rows, width = operands[-1].shape
    single = not isinstance(outs, tuple)
    shapes = [jax.ShapeDtypeStruct((rows, width), kind) for kind in ((outs,) if single else outs)]
    result = pl.pallas_call(
        body,
        out_shape=shapes[0] if single else tuple(shapes),
        in_specs=[SMEM if o.ndim == 1 else VMEM for o in operands],
        out_specs=VMEM if single else tuple(VMEM for _ in shapes),
        cost_estimate=pl.CostEstimate(
            flops=2 * rows * rows * width * dots,
            bytes_accessed=sum(o.size * o.dtype.itemsize for o in operands) + sum(4 * rows * width for _ in shapes),
            transcendentals=rows * rows * dots,
        ),
    )(*operands)
    return result


def shards(picture_encoder_embeds, caption_encoder_embeds, score_multiplier, score_offset_term):
    groups, halves = lax.axis_size("dp"), lax.axis_size("sub")
    chain = [group * halves + half for half in range(halves) for group in range(groups)]
    onward = [(chain[i], chain[(i + 1) % len(chain)]) for i in range(len(chain))]
    back = [(target, source) for source, target in onward]
    swap = [(0, 1), (1, 0)]
    to_right = lambda block: lax.ppermute(block, ("dp", "sub"), onward)
    to_left = lambda block: lax.ppermute(block, ("dp", "sub"), back)
    across = lambda block: lax.ppermute(block, "sub", swap)

    scalars = (score_multiplier.reshape(1), score_offset_term.reshape(1))
    text = call(normalize_kernel, BF16, (caption_encoder_embeds,), 0)
    image = call(normalize_kernel, BF16, (picture_encoder_embeds,), 0)
    far_text = across(text)
    left_image, right_image = to_right(image), to_left(image)
    left_text, right_text = to_right(text), to_left(text)
    far_left_text, far_right_text = to_right(far_text), to_left(far_text)
    far_dir = across(call(far_text_kernel, BF16, (*scalars, far_text, image, left_image, right_image), 6))
    image_dir, text_dir = call(
        near_kernel, (F32, F32), (*scalars, image, text, left_image, right_image, left_text, right_text), 12
    )
    image_grad = call(
        image_kernel,
        F32,
        (*scalars, image, image_dir, picture_encoder_embeds, far_text, far_left_text, far_right_text),
        6,
    )
    text_grad = call(text_kernel, F32, (text_dir, caption_encoder_embeds, far_dir), 0)
    return (image_grad, text_grad)


def solution(mesh):
    placed = (P(("dp", "sub"), None), P(("dp", "sub"), None), P(), P())
    return jax.shard_map(
        shards,
        mesh=mesh,
        in_specs=placed,
        out_specs=(P(("dp", "sub"), None), P(("dp", "sub"), None)),
        check_vma=False,
    )
```

time: 140 us -> 75.7 us (0.54)
  the two profiles are of different devices: /device:TPU:1 before, /device:TPU:16 now
where the time goes in v1:
time: 75.7 us; the launch traced here: 75.1 us
  starting transfers between devices  53 us (70%)
  Pallas kernels  16.8 us (22%)
  local copies, waits for them, and re-layouts  3.25 us (4%)
  between operations  2.09 us (3%)
    ppermute x3, starting transfers between devices, shards(): to_left = lambda block: lax.ppermute(block, ('dp', 'sub'), back)  34.6 us
    pallas_call x6, Pallas kernels, call(): pl.pallas_call(body, out_shape=shapes[0] if single else tuple(shapes), in...  16.8 us
    ppermute x2, starting transfers between devices, shards(): across = lambda block: lax.ppermute(block, 'sub', swap)  12.7 us
    ppermute x3, starting transfers between devices, shards(): to_right = lambda block: lax.ppermute(block, ('dp', 'sub'), onward)  5.75 us
    unnamed x16, local copies, waits for them, and re-layouts  3.25 us
  transfers between devices with their start and end apart: 8, of which 0 were waited for; matrix products, arithmetic and copies ran while one was open for 0% of the time, Pallas kernels for 15%

profile of v1, /device:TPU:16, one launch (start us, length us, event | category | flops | bytes accessed | tf_op | source)
XLA Modules:
  0.0 75.1 jit_solution(11356572687588322031)
XLA Ops:
  0.6 1.9 %shard_map.59.image_ref.own_ref = bf16[128,1152]{1,0:T(8,128)(2,1)} custom-call(f32[128,1152]{1,0:T(8,128)} %values_ref.6), custom_call_target="tpu_custom_call" | custom-call | bytes 1179648 | tf_op jit(solution)/shard_map/pallas_call | solution.py:98
  2.5 1.9 %collective-permute-start = (bf16[128,1152]{1,0:T(8,128)(2,1)}, bf16[128,1152]{1,0:T(8,128)(2,1)S(1)}, u32[]{:S(2)}, u32[]{:S(2)}) collective-permute-start(bf16[128,1152]{1,0:T(8,128)(2,1)} %shard_map.59.image_ref.own_ref), channel_id=1, source_target_pairs={{0,2},{2,4},{4,6},{6,8},{8,10},{10,12},{12,14},{14,16},{16,18},{18... | collective-permute-start | bytes 884744 | tf_op jit(solution)/shard_map/ppermute | solution.py:118
  4.5 18.8 %collective-permute-start.1 = (bf16[128,1152]{1,0:T(8,128)(2,1)}, bf16[128,1152]{1,0:T(8,128)(2,1)S(1)}, u32[]{:S(2)}, u32[]{:S(2)}) collective-permute-start(bf16[128,1152]{1,0:T(8,128)(2,1)} %shard_map.59.image_ref.own_ref), channel_id=1, source_target_pairs={{2,0},{4,2},{6,4},{8,6},{10,8},{12,10},{14,12},{16,14},{18,16},{20... | collective-permute-start | bytes 884744 | tf_op jit(solution)/shard_map/ppermute | solution.py:119
  23.3 1.9 %shard_map.60.text_ref = bf16[128,1152]{1,0:T(8,128)(2,1)} custom-call(f32[128,1152]{1,0:T(8,128)} %values_ref.7), custom_call_target="tpu_custom_call" | custom-call | bytes 1179648 | tf_op jit(solution)/shard_map/pallas_call | solution.py:98
  25.2 8.2 %collective-permute-start.4 = (bf16[128,1152]{1,0:T(8,128)(2,1)}, bf16[128,1152]{1,0:T(8,128)(2,1)S(1)}, u32[]{:S(2)}, u32[]{:S(2)}) collective-permute-start(bf16[128,1152]{1,0:T(8,128)(2,1)} %shard_map.60.text_ref), channel_id=1, source_target_pairs={{0,1},{1,0},{2,3},{3,2},{4,5},{5,4},{6,7},{7,6},{8,9},{9,8},{10,11... | collective-permute-start | bytes 884744 | tf_op jit(solution)/shard_map/ppermute | solution.py:120
  33.4 1.9 %collective-permute-start.2 = (bf16[128,1152]{1,0:T(8,128)(2,1)}, bf16[128,1152]{1,0:T(8,128)(2,1)S(1)}, u32[]{:S(2)}, u32[]{:S(2)}) collective-permute-start(bf16[128,1152]{1,0:T(8,128)(2,1)} %shard_map.60.text_ref), channel_id=1, source_target_pairs={{0,2},{2,4},{4,6},{6,8},{8,10},{10,12},{12,14},{14,16},{16,18},{18... | collective-permute-start | bytes 884744 | tf_op jit(solution)/shard_map/ppermute | solution.py:118
  35.3 7.9 %collective-permute-start.3 = (bf16[128,1152]{1,0:T(8,128)(2,1)}, bf16[128,1152]{1,0:T(8,128)(2,1)S(1)}, u32[]{:S(2)}, u32[]{:S(2)}) collective-permute-start(bf16[128,1152]{1,0:T(8,128)(2,1)} %shard_map.60.text_ref), channel_id=1, source_target_pairs={{2,0},{4,2},{6,4},{8,6},{10,8},{12,10},{14,12},{16,14},{18,16},{20... | collective-permute-start | bytes 884744 | tf_op jit(solution)/shard_map/ppermute | solution.py:119
  44.5 0.0 collective-permute-done.left_image_ref.left_ref
  44.5 0.0 copy-start.1
  44.5 0.0 collective-permute-done.1.right_image_ref.right_ref
  44.5 0.0 copy-start.2
  44.5 0.0 collective-permute-done.4.far_ref
  44.5 0.0 copy-start
  44.5 0.7 copy-done.1
  45.2 0.1 copy-done.2
  45.3 0.1 copy-done
  45.5 2.9 %shard_map.63 = bf16[128,1152]{1,0:T(8,128)(2,1)} custom-call(f32[1]{0:T(128)} %bitcast.4.scale_ref, f32[1]{0:T(128)} %bitcast.7.offset_ref, bf16[128,1152]{1,0:T(8,128)(2,1)} %copy-done, bf16[128,1152]{1,0:T(8,128)(2,1)} %shard_map.59.image_ref.own_ref, bf16[128,1152]{1,0:T(8,128)(2,1)} %copy-done.1, bf16[128,1152]{1,0:T(8,128)(2,1)} %copy-done.2), custom_call_target="tpu_custom_call" | custom-call | flops 226492416 | bytes 1769480 | tf_op jit(solution)/shard_map/pallas_call | solution.py:98
  48.4 4.5 %collective-permute-start.7 = (bf16[128,1152]{1,0:T(8,128)(2,1)}, bf16[128,1152]{1,0:T(8,128)(2,1)S(1)}, u32[]{:S(2)}, u32[]{:S(2)}) collective-permute-start(bf16[128,1152]{1,0:T(8,128)(2,1)} %shard_map.63), channel_id=1, source_target_pairs={{0,1},{1,0},{2,3},{3,2},{4,5},{5,4},{6,7},{7,6},{8,9},{9,8},{10,11... | collective-permute-start | bytes 884744 | tf_op jit(solution)/shard_map/ppermute | solution.py:120
  52.9 1.9 %collective-permute-start.5 = (bf16[128,1152]{1,0:T(8,128)(2,1)}, bf16[128,1152]{1,0:T(8,128)(2,1)S(1)}, u32[]{:S(2)}, u32[]{:S(2)}) collective-permute-start(bf16[128,1152]{1,0:T(8,128)(2,1)} %copy-done), channel_id=1, source_target_pairs={{0,2},{2,4},{4,6},{6,8},{8,10},{10,12},{12,14},{14,16},{16,18},{18... | collective-permute-start | bytes 884744 | tf_op jit(solution)/shard_map/ppermute | solution.py:118
  54.8 7.9 %collective-permute-start.6 = (bf16[128,1152]{1,0:T(8,128)(2,1)}, bf16[128,1152]{1,0:T(8,128)(2,1)S(1)}, u32[]{:S(2)}, u32[]{:S(2)}) collective-permute-start(bf16[128,1152]{1,0:T(8,128)(2,1)} %copy-done), channel_id=1, source_target_pairs={{2,0},{4,2},{6,4},{8,6},{10,8},{12,10},{14,12},{16,14},{18,16},{20... | collective-permute-start | bytes 884744 | tf_op jit(solution)/shard_map/ppermute | solution.py:119
  62.7 0.0 collective-permute-done.2.left_text_ref
  62.7 0.0 copy-start.3
  62.7 0.0 collective-permute-done.3.right_text_ref
  62.7 0.0 copy-start.4
  62.7 0.7 copy-done.3
  63.4 0.1 copy-done.4
  63.5 3.9 %shard_map.61 = (f32[128,1152]{1,0:T(8,128)}, f32[128,1152]{1,0:T(8,128)}) custom-call(f32[1]{0:T(128)} %bitcast.2.scale_ref, f32[1]{0:T(128)} %bitcast.5.offset_ref, bf16[128,1152]{1,0:T(8,128)(2,1)} %shard_map.59.image_ref.own_ref, bf16[128,1152]{1,0:T(8,128)(2,1)} %shard_map.60.text_ref, bf16[128,1152]{1,0:T(8,128)(2,1)} %copy-done.1, ...), custom_call_target="tpu_custom_call" | custom-call | flops 452984832 | bytes 2949128 | tf_op jit(solution)/shard_map/pallas_call | solution.py:98
  67.5 0.0 collective-permute-done.7.far_dir_ref
  67.5 0.0 copy-start.7
  67.5 0.7 copy-done.7
  68.2 2.4 %shard_map.64 = f32[128,1152]{1,0:T(8,128)} custom-call(f32[128,1152]{1,0:T(8,128)} %get-tuple-element.5.near_dir_ref, f32[128,1152]{1,0:T(8,128)} %values_ref.7, bf16[128,1152]{1,0:T(8,128)(2,1)} %copy-done.7), custom_call_target="tpu_custom_call" | custom-call | bytes 2064384 | tf_op jit(solution)/shard_map/pallas_call | solution.py:98
  70.6 0.0 collective-permute-done.5.far_left_ref
  70.6 0.0 copy-start.5
  70.6 0.0 collective-permute-done.6.far_right_ref
  70.6 0.0 copy-start.6
  70.6 0.7 copy-done.5
  71.3 0.1 copy-done.6
  71.4 3.7 %shard_map.62 = f32[128,1152]{1,0:T(8,128)} custom-call(f32[1]{0:T(128)} %bitcast.3.scale_ref, f32[1]{0:T(128)} %bitcast.6.offset_ref, bf16[128,1152]{1,0:T(8,128)(2,1)} %shard_map.59.image_ref.own_ref, f32[128,1152]{1,0:T(8,128)} %get-tuple-element.4.near_dir_ref, f32[128,1152]{1,0:T(8,128)} %values_ref.6, bf16[128,1152]{1,0:T(8,128)(2,1)} %copy-done, ...), custom_call_target="tpu_custom_call" | custom-call | flops 226492416 | bytes 2949128 | tf_op jit(solution)/shard_map/pallas_call | solution.py:98
Async XLA Ops:
  2.5 41.9 %collective-permute-start = (bf16[128,1152]{1,0:T(8,128)(2,1)}, bf16[128,1152]{1,0:T(8,128)(2,1)S(1)}, u32[]{:S(2)}, u32[]{:S(2)}) collective-permute-start(bf16[128,1152]{1,0:T(8,128)(2,1)} %shard_map.59.image_ref.own_ref), channel_id=1, source_target_pairs={{0,2},{2,4},{4,6},{6,8},{8,10},{10,12},{12,14},{14,16},{16,18},{18... | collective-permute-start | bytes 884744 | tf_op jit(solution)/shard_map/ppermute | solution.py:118
  4.5 40.1 %collective-permute-start.1 = (bf16[128,1152]{1,0:T(8,128)(2,1)}, bf16[128,1152]{1,0:T(8,128)(2,1)S(1)}, u32[]{:S(2)}, u32[]{:S(2)}) collective-permute-start(bf16[128,1152]{1,0:T(8,128)(2,1)} %shard_map.59.image_ref.own_ref), channel_id=1, source_target_pairs={{2,0},{4,2},{6,4},{8,6},{10,8},{12,10},{14,12},{16,14},{18,16},{20... | collective-permute-start | bytes 884744 | tf_op jit(solution)/shard_map/ppermute | solution.py:119
  25.2 19.3 %collective-permute-start.4 = (bf16[128,1152]{1,0:T(8,128)(2,1)}, bf16[128,1152]{1,0:T(8,128)(2,1)S(1)}, u32[]{:S(2)}, u32[]{:S(2)}) collective-permute-start(bf16[128,1152]{1,0:T(8,128)(2,1)} %shard_map.60.text_ref), channel_id=1, source_target_pairs={{0,1},{1,0},{2,3},{3,2},{4,5},{5,4},{6,7},{7,6},{8,9},{9,8},{10,11... | collective-permute-start | bytes 884744 | tf_op jit(solution)/shard_map/ppermute | solution.py:120
  33.4 29.3 %collective-permute-start.2 = (bf16[128,1152]{1,0:T(8,128)(2,1)}, bf16[128,1152]{1,0:T(8,128)(2,1)S(1)}, u32[]{:S(2)}, u32[]{:S(2)}) collective-permute-start(bf16[128,1152]{1,0:T(8,128)(2,1)} %shard_map.60.text_ref), channel_id=1, source_target_pairs={{0,2},{2,4},{4,6},{6,8},{8,10},{10,12},{12,14},{14,16},{16,18},{18... | collective-permute-start | bytes 884744 | tf_op jit(solution)/shard_map/ppermute | solution.py:118
  35.3 27.4 %collective-permute-start.3 = (bf16[128,1152]{1,0:T(8,128)(2,1)}, bf16[128,1152]{1,0:T(8,128)(2,1)S(1)}, u32[]{:S(2)}, u32[]{:S(2)}) collective-permute-start(bf16[128,1152]{1,0:T(8,128)(2,1)} %shard_map.60.text_ref), channel_id=1, source_target_pairs={{2,0},{4,2},{6,4},{8,6},{10,8},{12,10},{14,12},{16,14},{18,16},{20... | collective-permute-start | bytes 884744 | tf_op jit(solution)/shard_map/ppermute | solution.py:119
  44.5 0.7 copy-start.1
  44.5 0.8 %copy-start.2 = (bf16[128,1152]{1,0:T(8,128)(2,1)}, bf16[128,1152]{1,0:T(8,128)(2,1)S(1)}, u32[]{:S(2)}) copy-start(bf16[128,1152]{1,0:T(8,128)(2,1)S(1)} %collective-permute-done.1.right_image_ref.right_ref) | copy-start | bytes 884740
  44.5 0.9 %copy-start = (bf16[128,1152]{1,0:T(8,128)(2,1)}, bf16[128,1152]{1,0:T(8,128)(2,1)S(1)}, u32[]{:S(2)}) copy-start(bf16[128,1152]{1,0:T(8,128)(2,1)S(1)} %collective-permute-done.4.far_ref) | copy-start | bytes 884740
  48.4 19.1 %collective-permute-start.7 = (bf16[128,1152]{1,0:T(8,128)(2,1)}, bf16[128,1152]{1,0:T(8,128)(2,1)S(1)}, u32[]{:S(2)}, u32[]{:S(2)}) collective-permute-start(bf16[128,1152]{1,0:T(8,128)(2,1)} %shard_map.63), channel_id=1, source_target_pairs={{0,1},{1,0},{2,3},{3,2},{4,5},{5,4},{6,7},{7,6},{8,9},{9,8},{10,11... | collective-permute-start | bytes 884744 | tf_op jit(solution)/shard_map/ppermute | solution.py:120
  52.9 17.7 %collective-permute-start.5 = (bf16[128,1152]{1,0:T(8,128)(2,1)}, bf16[128,1152]{1,0:T(8,128)(2,1)S(1)}, u32[]{:S(2)}, u32[]{:S(2)}) collective-permute-start(bf16[128,1152]{1,0:T(8,128)(2,1)} %copy-done), channel_id=1, source_target_pairs={{0,2},{2,4},{4,6},{6,8},{8,10},{10,12},{12,14},{14,16},{16,18},{18... | collective-permute-start | bytes 884744 | tf_op jit(solution)/shard_map/ppermute | solution.py:118
  54.8 15.8 %collective-permute-start.6 = (bf16[128,1152]{1,0:T(8,128)(2,1)}, bf16[128,1152]{1,0:T(8,128)(2,1)S(1)}, u32[]{:S(2)}, u32[]{:S(2)}) collective-permute-start(bf16[128,1152]{1,0:T(8,128)(2,1)} %copy-done), channel_id=1, source_target_pairs={{2,0},{4,2},{6,4},{8,6},{10,8},{12,10},{14,12},{16,14},{18,16},{20... | collective-permute-start | bytes 884744 | tf_op jit(solution)/shard_map/ppermute | solution.py:119
  62.7 0.7 copy-start.3
  62.7 0.8 %copy-start.4 = (bf16[128,1152]{1,0:T(8,128)(2,1)}, bf16[128,1152]{1,0:T(8,128)(2,1)S(1)}, u32[]{:S(2)}) copy-start(bf16[128,1152]{1,0:T(8,128)(2,1)S(1)} %collective-permute-done.3.right_text_ref) | copy-start | bytes 884740
  67.5 0.7 copy-start.7
  70.6 0.7 copy-start.5
  70.6 0.8 %copy-start.6 = (bf16[128,1152]{1,0:T(8,128)(2,1)}, bf16[128,1152]{1,0:T(8,128)(2,1)S(1)}, u32[]{:S(2)}) copy-start(bf16[128,1152]{1,0:T(8,128)(2,1)S(1)} %collective-permute-done.6.far_right_ref) | copy-start | bytes 884740

commit v2 on v0

v2 whole, which is shorter than its diff:
```python
import jax
import jax.numpy as jnp
from jax import lax
from jax.sharding import PartitionSpec as P

BF16 = jnp.bfloat16
F32 = jnp.float32


def times_transposed(a, b):
    return lax.dot_general(a, b, (((1,), (1,)), ((), ())), preferred_element_type=F32)


def times(a, b):
    return lax.dot_general(a, b, (((1,), (0,)), ((), ())), preferred_element_type=F32)


def normalize(values):
    inverse = lax.rsqrt(jnp.sum(values * values, axis=-1, keepdims=True) + 1e-06)
    return (values * inverse).astype(BF16), inverse


def backward_norm(values, inverse, direction):
    unit = values * inverse
    return (direction - unit * jnp.sum(unit * direction, axis=-1, keepdims=True)) * inverse


def transposed_times(a, b):
    return lax.dot_general(a, b, (((0,), (0,)), ((), ())), preferred_element_type=F32)


def band_coeffs(scale, offset, images, texts, rows):
    scores = scale * times_transposed(images, texts) + offset
    image_ids = lax.broadcasted_iota(jnp.int32, scores.shape, 0)
    text_ids = lax.broadcasted_iota(jnp.int32, scores.shape, 1)
    label = jnp.where((image_ids == text_ids) & (image_ids < rows), F32(1.0), F32(-1.0))
    coeffs = (-label * scale * jax.nn.sigmoid(-label * scores)).astype(BF16)
    return lax.optimization_barrier(coeffs)


def shards(picture_encoder_embeds, caption_encoder_embeds, score_multiplier, score_offset_term):
    groups, halves = lax.axis_size("dp"), lax.axis_size("sub")
    chain = [group * halves + half for half in range(halves) for group in range(groups)]
    onward = [(chain[i], chain[(i + 1) % len(chain)]) for i in range(len(chain))]
    back = [(target, source) for source, target in onward]
    swap = [(0, 1), (1, 0)]
    to_right = lambda block: lax.ppermute(block, ("dp", "sub"), onward)
    to_left = lambda block: lax.ppermute(block, ("dp", "sub"), back)
    across = lambda block: lax.ppermute(block, "sub", swap)
    rows = picture_encoder_embeds.shape[0]
    after = lambda value, earlier: lax.optimization_barrier((value, earlier))[0]

    text, text_inverse = normalize(caption_encoder_embeds)
    far_text = across(text)
    image, image_inverse = normalize(after(picture_encoder_embeds, text))
    left_image, right_image = to_right(image), to_left(image)
    texts = jnp.concatenate([text, far_text])
    own = band_coeffs(score_multiplier, score_offset_term, image, texts, rows)
    left_image, right_image, own = lax.optimization_barrier((left_image, right_image, own))
    sides = jnp.concatenate([left_image, right_image])
    side_coeffs = band_coeffs(score_multiplier, score_offset_term, sides, texts, 0)
    images = jnp.concatenate([image, sides])
    coeffs = jnp.concatenate([own, side_coeffs])
    far_dir = transposed_times(coeffs[:, rows:], images).astype(BF16)
    coeffs, far_dir = lax.optimization_barrier((coeffs, far_dir))
    far_dir = across(far_dir)
    right_dir = times(coeffs[2 * rows :], texts).astype(BF16)
    from_left = to_right(right_dir)
    left_dir = times(coeffs[rows : 2 * rows], texts).astype(BF16)
    from_right = to_left(left_dir)
    text_dir = transposed_times(coeffs[:, :rows], images) + far_dir.astype(F32)
    text_grad = backward_norm(caption_encoder_embeds, text_inverse, text_dir)
    from_left, from_right, text_grad = lax.optimization_barrier((from_left, from_right, text_grad))
    image_dir = times(coeffs[:rows], texts) + from_left.astype(F32) + from_right.astype(F32)
    image_grad = backward_norm(picture_encoder_embeds, image_inverse, image_dir)
    return (image_grad, text_grad)


def solution(mesh):
    placed = (P(("dp", "sub"), None), P(("dp", "sub"), None), P(), P())
    return jax.shard_map(
        shards,
        mesh=mesh,
        in_specs=placed,
        out_specs=(P(("dp", "sub"), None), P(("dp", "sub"), None)),
        check_vma=False,
    )
```

time: 140 us -> 64.1 us (0.46)
  the two profiles are of different devices: /device:TPU:1 before, /device:TPU:64 now
where the time goes in v2:
time: 64.1 us; the launch traced here: 63.8 us
  starting transfers between devices  42.5 us (66%)
  waiting for transfers between devices  13.1 us (20%)
  other arithmetic  3.6 us (6%)
  matrix products  2.48 us (4%)
  between operations  2.1 us (3%)
    ppermute x2, starting transfers between devices, shards(): to_left = lambda block: lax.ppermute(block, ('dp', 'sub'), back)  19.6 us
    ppermute x2, starting transfers between devices, shards(): across = lambda block: lax.ppermute(block, 'sub', swap)  19.1 us
    ppermute x2, waiting for transfers between devices, shards(): to_right = lambda block: lax.ppermute(block, ('dp', 'sub'), onward)  12.1 us
    ppermute x2, starting transfers between devices, shards(): to_right = lambda block: lax.ppermute(block, ('dp', 'sub'), onward)  3.84 us
    mul x2, other arithmetic, backward_norm(): (direction - unit * jnp.sum(unit * direction, axis=-1, keepdims=True)) *...  1.99 us
    reduce_sum x2, other arithmetic, normalize(): jnp.sum(values * values, axis=-1, keepdims=True) + 1e-06  1.37 us
  transfers between devices with their start and end apart: 6, of which 4 were waited for; matrix products, arithmetic and copies ran while one was open for 4% of the time, Pallas kernels for 0%

profile of v2, /device:TPU:64, one launch (start us, length us, event | category | flops | bytes accessed | tf_op | source)
XLA Modules:
  0.0 63.8 jit_solution(18204767652552529626)
XLA Ops:
  0.6 0.0 copy-start.1
  0.6 1.2 %multiply_reduce_fusion.3 = f32[128]{0:T(128)S(1)} fusion(f32[128,1152]{1,0:T(8,128)} %param.5), kind=kLoop, calls=%fused_computation.34 | loop fusion | flops 294784 | bytes 590336 | tf_op jit(solution)/shard_map/reduce_sum | solution.py:19
  1.9 0.0 copy-start
  1.9 0.0 copy-done.1
  1.9 0.1 multiply_convert_fusion.1
  2.0 14.3 %collective-permute-start.2 = (bf16[128,1152]{1,0:T(8,128)(2,1)S(1)}, bf16[128,1152]{1,0:T(8,128)(2,1)S(1)}, u32[]{:S(2)}, u32[]{:S(2)}) collective-permute-start(bf16[128,1152]{1,0:T(8,128)(2,1)S(1)} %multiply_convert_fusion.1), channel_id=1, source_target_pairs={{0,1},{1,0},{2,3},{3,2},{4,5},{5,4},{6,7},{7,6},{8,9},{9,8},{10,11... | collective-permute-start | bytes 884744 | tf_op jit(solution)/shard_map/ppermute | solution.py:49
  16.4 0.0 copy-done
  16.4 0.1 multiply_reduce_fusion.2
  16.5 0.1 multiply_convert_fusion
  16.6 1.9 %collective-permute-start = (bf16[128,1152]{1,0:T(8,128)(2,1)S(1)}, bf16[128,1152]{1,0:T(8,128)(2,1)S(1)}, u32[]{:S(2)}, u32[]{:S(2)}) collective-permute-start(bf16[128,1152]{1,0:T(8,128)(2,1)S(1)} %multiply_convert_fusion), channel_id=1, source_target_pairs={{0,2},{2,4},{4,6},{6,8},{8,10},{10,12},{12,14},{14,16},{16,18},{18... | collective-permute-start | bytes 884744 | tf_op jit(solution)/shard_map/ppermute | solution.py:47
  18.6 9.9 %collective-permute-start.1 = (bf16[128,1152]{1,0:T(8,128)(2,1)S(1)}, bf16[128,1152]{1,0:T(8,128)(2,1)S(1)}, u32[]{:S(2)}, u32[]{:S(2)}) collective-permute-start(bf16[128,1152]{1,0:T(8,128)(2,1)S(1)} %multiply_convert_fusion), channel_id=1, source_target_pairs={{2,0},{4,2},{6,4},{8,6},{10,8},{12,10},{14,12},{16,14},{18,16},{20... | collective-permute-start | bytes 884744 | tf_op jit(solution)/shard_map/ppermute | solution.py:48
  29.7 0.0 collective-permute-done.2
  29.8 0.4 fusion.15
  30.1 2.6 %collective-permute-done = bf16[128,1152]{1,0:T(8,128)(2,1)S(1)} collective-permute-done((bf16[128,1152]{1,0:T(8,128)(2,1)S(1)}, bf16[128,1152]{1,0:T(8,128)(2,1)S(1)}, u32[]{:S(2)}, u32[]{:S(2)}) %collective-permute-start) | collective-permute-done | bytes 294944 | tf_op jit(solution)/shard_map/ppermute | solution.py:47
  32.7 0.5 collective-permute-done.1
  33.2 0.4 fusion.7
  33.6 0.4 convolution_convert_fusion.2
  34.0 4.7 %collective-permute-start.5 = (bf16[128,1152]{1,0:T(8,128)(2,1)S(1)}, bf16[128,1152]{1,0:T(8,128)(2,1)S(1)}, u32[]{:S(2)}, u32[]{:S(2)}) collective-permute-start(bf16[128,1152]{1,0:T(8,128)(2,1)S(1)} %convolution_convert_fusion.2), channel_id=1, source_target_pairs={{0,1},{1,0},{2,3},{3,2},{4,5},{5,4},{6,7},{7,6},{8,9},{9,8},{10,11... | collective-permute-start | bytes 884744 | tf_op jit(solution)/shard_map/ppermute | solution.py:49
  38.7 0.2 convolution_convert_fusion
  39.0 9.7 %collective-permute-start.4 = (bf16[128,1152]{1,0:T(8,128)(2,1)S(1)}, bf16[128,1152]{1,0:T(8,128)(2,1)S(1)}, u32[]{:S(2)}, u32[]{:S(2)}) collective-permute-start(bf16[128,1152]{1,0:T(8,128)(2,1)S(1)} %convolution_convert_fusion), channel_id=1, source_target_pairs={{2,0},{4,2},{6,4},{8,6},{10,8},{12,10},{14,12},{16,14},{18,16},{20... | collective-permute-start | bytes 884744 | tf_op jit(solution)/shard_map/ppermute | solution.py:48
  48.7 0.2 convolution_convert_fusion.1
  49.0 1.9 %collective-permute-start.3 = (bf16[128,1152]{1,0:T(8,128)(2,1)S(1)}, bf16[128,1152]{1,0:T(8,128)(2,1)S(1)}, u32[]{:S(2)}, u32[]{:S(2)}) collective-permute-start(bf16[128,1152]{1,0:T(8,128)(2,1)S(1)} %convolution_convert_fusion.1), channel_id=1, source_target_pairs={{0,2},{2,4},{4,6},{6,8},{8,10},{10,12},{12,14},{14,16},{16,18},{18... | collective-permute-start | bytes 884744 | tf_op jit(solution)/shard_map/ppermute | solution.py:47
  50.9 0.0 collective-permute-done.5
  50.9 0.5 multiply_reduce_fusion.1
  51.4 1.0 %subtract_multiply_fusion.1 = f32[128,1152]{1,0:T(8,128)} fusion(f32[128,1152]{1,0:T(8,128)S(1)} %copy-done.1, f32[128,1152]{1,0:T(8,128)S(1)} %get-tuple-element.21, bf16[128,1152]{1,0:T(8,128)(2,1)S(1)} %collective-permute-done.5, f32[128]{0:T(128)S(1)} %get-tuple-element.20, f32[128]{0:T(128)S(1)} %add_rsqrt_fusion.1), kind=kLoop, calls=%fused_computation.29 | loop fusion | flops 884736 | bytes 2065408 | tf_op jit(solution)/shard_map/mul | solution.py:25
  52.4 0.5 collective-permute-done.4
  52.9 9.5 %collective-permute-done.3 = bf16[128,1152]{1,0:T(8,128)(2,1)S(1)} collective-permute-done((bf16[128,1152]{1,0:T(8,128)(2,1)S(1)}, bf16[128,1152]{1,0:T(8,128)(2,1)S(1)}, u32[]{:S(2)}, u32[]{:S(2)}) %collective-permute-start.3) | collective-permute-done | bytes 294944 | tf_op jit(solution)/shard_map/ppermute | solution.py:47
  62.4 0.4 multiply_reduce_fusion
  62.8 1.0 %subtract_multiply_fusion = f32[128,1152]{1,0:T(8,128)} fusion(f32[128,1152]{1,0:T(8,128)S(1)} %get-tuple-element.23, f32[128,1152]{1,0:T(8,128)S(1)} %copy-done, f32[128]{0:T(128)S(1)} %get-tuple-element.22, f32[128]{0:T(128)S(1)} %add_rsqrt_fusion), kind=kLoop, calls=%fused_computation.27 | loop fusion | flops 589824 | bytes 1770496 | tf_op jit(solution)/shard_map/mul | solution.py:25
  (4 shorter events, 0.0 us)
Async XLA Ops:
  0.6 1.3 %copy-start.1 = (f32[128,1152]{1,0:T(8,128)S(1)}, f32[128,1152]{1,0:T(8,128)}, u32[]{:S(2)}) copy-start(f32[128,1152]{1,0:T(8,128)} %param.5) | copy-start | bytes 1769476
  1.9 14.5 %copy-start = (f32[128,1152]{1,0:T(8,128)S(1)}, f32[128,1152]{1,0:T(8,128)}, u32[]{:S(2)}) copy-start(f32[128,1152]{1,0:T(8,128)} %param.4) | copy-start | bytes 1769476
  2.0 27.7 %collective-permute-start.2 = (bf16[128,1152]{1,0:T(8,128)(2,1)S(1)}, bf16[128,1152]{1,0:T(8,128)(2,1)S(1)}, u32[]{:S(2)}, u32[]{:S(2)}) collective-permute-start(bf16[128,1152]{1,0:T(8,128)(2,1)S(1)} %multiply_convert_fusion.1), channel_id=1, source_target_pairs={{0,1},{1,0},{2,3},{3,2},{4,5},{5,4},{6,7},{7,6},{8,9},{9,8},{10,11... | collective-permute-start | bytes 884744 | tf_op jit(solution)/shard_map/ppermute | solution.py:49
  16.6 16.1 %collective-permute-start = (bf16[128,1152]{1,0:T(8,128)(2,1)S(1)}, bf16[128,1152]{1,0:T(8,128)(2,1)S(1)}, u32[]{:S(2)}, u32[]{:S(2)}) collective-permute-start(bf16[128,1152]{1,0:T(8,128)(2,1)S(1)} %multiply_convert_fusion), channel_id=1, source_target_pairs={{0,2},{2,4},{4,6},{6,8},{8,10},{10,12},{12,14},{14,16},{16,18},{18... | collective-permute-start | bytes 884744 | tf_op jit(solution)/shard_map/ppermute | solution.py:47
  18.6 14.6 %collective-permute-start.1 = (bf16[128,1152]{1,0:T(8,128)(2,1)S(1)}, bf16[128,1152]{1,0:T(8,128)(2,1)S(1)}, u32[]{:S(2)}, u32[]{:S(2)}) collective-permute-start(bf16[128,1152]{1,0:T(8,128)(2,1)S(1)} %multiply_convert_fusion), channel_id=1, source_target_pairs={{2,0},{4,2},{6,4},{8,6},{10,8},{12,10},{14,12},{16,14},{18,16},{20... | collective-permute-start | bytes 884744 | tf_op jit(solution)/shard_map/ppermute | solution.py:48
  34.0 16.9 %collective-permute-start.5 = (bf16[128,1152]{1,0:T(8,128)(2,1)S(1)}, bf16[128,1152]{1,0:T(8,128)(2,1)S(1)}, u32[]{:S(2)}, u32[]{:S(2)}) collective-permute-start(bf16[128,1152]{1,0:T(8,128)(2,1)S(1)} %convolution_convert_fusion.2), channel_id=1, source_target_pairs={{0,1},{1,0},{2,3},{3,2},{4,5},{5,4},{6,7},{7,6},{8,9},{9,8},{10,11... | collective-permute-start | bytes 884744 | tf_op jit(solution)/shard_map/ppermute | solution.py:49
  39.0 14.0 %collective-permute-start.4 = (bf16[128,1152]{1,0:T(8,128)(2,1)S(1)}, bf16[128,1152]{1,0:T(8,128)(2,1)S(1)}, u32[]{:S(2)}, u32[]{:S(2)}) collective-permute-start(bf16[128,1152]{1,0:T(8,128)(2,1)S(1)} %convolution_convert_fusion), channel_id=1, source_target_pairs={{2,0},{4,2},{6,4},{8,6},{10,8},{12,10},{14,12},{16,14},{18,16},{20... | collective-permute-start | bytes 884744 | tf_op jit(solution)/shard_map/ppermute | solution.py:48
  49.0 13.5 %collective-permute-start.3 = (bf16[128,1152]{1,0:T(8,128)(2,1)S(1)}, bf16[128,1152]{1,0:T(8,128)(2,1)S(1)}, u32[]{:S(2)}, u32[]{:S(2)}) collective-permute-start(bf16[128,1152]{1,0:T(8,128)(2,1)S(1)} %convolution_convert_fusion.1), channel_id=1, source_target_pairs={{0,2},{2,4},{4,6},{6,8},{8,10},{10,12},{12,14},{14,16},{16,18},{18... | collective-permute-start | bytes 884744 | tf_op jit(solution)/shard_map/ppermute | solution.py:47

commit v3 on v2

--- a/solution.py
+++ b/solution.py
@@ -53,25 +53,28 @@
     text, text_inverse = normalize(caption_encoder_embeds)
     far_text = across(text)
     image, image_inverse = normalize(after(picture_encoder_embeds, text))
-    left_image, right_image = to_right(image), to_left(image)
+    right_image, left_image = to_left(image), to_right(image)
     texts = jnp.concatenate([text, far_text])
     own = band_coeffs(score_multiplier, score_offset_term, image, texts, rows)
-    left_image, right_image, own = lax.optimization_barrier((left_image, right_image, own))
+    right_image, left_image, own = lax.optimization_barrier((right_image, left_image, own))
     sides = jnp.concatenate([left_image, right_image])
     side_coeffs = band_coeffs(score_multiplier, score_offset_term, sides, texts, 0)
     images = jnp.concatenate([image, sides])
     coeffs = jnp.concatenate([own, side_coeffs])
-    far_dir = transposed_times(coeffs[:, rows:], images).astype(BF16)
-    coeffs, far_dir = lax.optimization_barrier((coeffs, far_dir))
-    far_dir = across(far_dir)
     right_dir = times(coeffs[2 * rows :], texts).astype(BF16)
     from_left = to_right(right_dir)
-    left_dir = times(coeffs[rows : 2 * rows], texts).astype(BF16)
+    far_coeffs = after(coeffs[:, rows:], right_dir)
+    far_dir = transposed_times(far_coeffs, images).astype(BF16)
+    left_coeffs = after(coeffs[rows : 2 * rows], far_dir)
+    far_dir = across(far_dir)
+    left_dir = times(left_coeffs, texts).astype(BF16)
     from_right = to_left(left_dir)
+    image_part = times(coeffs[:rows], texts) + from_left.astype(F32)
+    far_dir, image_part = lax.optimization_barrier((far_dir, image_part))
     text_dir = transposed_times(coeffs[:, :rows], images) + far_dir.astype(F32)
     text_grad = backward_norm(caption_encoder_embeds, text_inverse, text_dir)
-    from_left, from_right, text_grad = lax.optimization_barrier((from_left, from_right, text_grad))
-    image_dir = times(coeffs[:rows], texts) + from_left.astype(F32) + from_right.astype(F32)
+    from_right, text_grad = lax.optimization_barrier((from_right, text_grad))
+    image_dir = image_part + from_right.astype(F32)
     image_grad = backward_norm(picture_encoder_embeds, image_inverse, image_dir)
     return (image_grad, text_grad)
 

time: 64.1 us -> 57.7 us (0.900)
  the two profiles are of different devices: /device:TPU:64 before, /device:TPU:12 now
where the time goes in v3:
time: 57.7 us; the launch traced here: 57.4 us
  starting transfers between devices  38.8 us (67%)
  waiting for transfers between devices  10.3 us (18%)
  other arithmetic  3.8 us (7%)
  matrix products  2.35 us (4%)
  between operations  2.11 us (4%)
    ppermute x2, starting transfers between devices, shards(): to_left = lambda block: lax.ppermute(block, ('dp', 'sub'), back)  24.4 us
    ppermute x2, starting transfers between devices, shards(): across = lambda block: lax.ppermute(block, 'sub', swap)  10.5 us
    ppermute x2, waiting for transfers between devices, shards(): across = lambda block: lax.ppermute(block, 'sub', swap)  7.76 us
    ppermute x2, starting transfers between devices, shards(): to_right = lambda block: lax.ppermute(block, ('dp', 'sub'), onward)  3.84 us
    mul x2, other arithmetic, backward_norm(): (direction - unit * jnp.sum(unit * direction, axis=-1, keepdims=True)) *...  1.98 us
    ppermute x2, waiting for transfers between devices, shards(): to_left = lambda block: lax.ppermute(block, ('dp', 'sub'), back)  1.76 us
    reduce_sum x2, other arithmetic, normalize(): jnp.sum(values * values, axis=-1, keepdims=True) + 1e-06  1.37 us
  transfers between devices with their start and end apart: 6, of which 3 were waited for; matrix products, arithmetic and copies ran while one was open for 5% of the time, Pallas kernels for 0%

profile of v3, /device:TPU:12, one launch (start us, length us, event | category | flops | bytes accessed | tf_op | source)
XLA Modules:
  0.0 57.4 jit_solution(3967231872836686361)
XLA Ops:
  0.6 0.0 copy-start.1
  0.6 1.2 %multiply_reduce_fusion.3 = f32[128]{0:T(128)S(1)} fusion(f32[128,1152]{1,0:T(8,128)} %param.5), kind=kLoop, calls=%fused_computation.34 | loop fusion | flops 294784 | bytes 590336 | tf_op jit(solution)/shard_map/reduce_sum | solution.py:19
  1.9 0.0 copy-start
  1.9 0.0 copy-done.1
  1.9 0.1 multiply_convert_fusion.1
  2.0 8.3 %collective-permute-start.2 = (bf16[128,1152]{1,0:T(8,128)(2,1)S(1)}, bf16[128,1152]{1,0:T(8,128)(2,1)S(1)}, u32[]{:S(2)}, u32[]{:S(2)}) collective-permute-start(bf16[128,1152]{1,0:T(8,128)(2,1)S(1)} %multiply_convert_fusion.1), channel_id=1, source_target_pairs={{0,1},{1,0},{2,3},{3,2},{4,5},{5,4},{6,7},{7,6},{8,9},{9,8},{10,11... | collective-permute-start | bytes 884744 | tf_op jit(solution)/shard_map/ppermute | solution.py:49
  10.4 0.0 copy-done
  10.4 0.1 multiply_reduce_fusion.2
  10.5 0.1 multiply_convert_fusion
  10.6 1.9 %collective-permute-start.1 = (bf16[128,1152]{1,0:T(8,128)(2,1)S(1)}, bf16[128,1152]{1,0:T(8,128)(2,1)S(1)}, u32[]{:S(2)}, u32[]{:S(2)}) collective-permute-start(bf16[128,1152]{1,0:T(8,128)(2,1)S(1)} %multiply_convert_fusion), channel_id=1, source_target_pairs={{0,2},{2,4},{4,6},{6,8},{8,10},{10,12},{12,14},{14,16},{16,18},{18... | collective-permute-start | bytes 884744 | tf_op jit(solution)/shard_map/ppermute | solution.py:47
  12.5 17.4 %collective-permute-start = (bf16[128,1152]{1,0:T(8,128)(2,1)S(1)}, bf16[128,1152]{1,0:T(8,128)(2,1)S(1)}, u32[]{:S(2)}, u32[]{:S(2)}) collective-permute-start(bf16[128,1152]{1,0:T(8,128)(2,1)S(1)} %multiply_convert_fusion), channel_id=1, source_target_pairs={{2,0},{4,2},{6,4},{8,6},{10,8},{12,10},{14,12},{16,14},{18,16},{20... | collective-permute-start | bytes 884744 | tf_op jit(solution)/shard_map/ppermute | solution.py:48
  31.3 0.0 collective-permute-done.2
  31.3 0.4 fusion.14
  31.7 0.8 %collective-permute-done.1 = bf16[128,1152]{1,0:T(8,128)(2,1)S(1)} collective-permute-done((bf16[128,1152]{1,0:T(8,128)(2,1)S(1)}, bf16[128,1152]{1,0:T(8,128)(2,1)S(1)}, u32[]{:S(2)}, u32[]{:S(2)}) %collective-permute-start.1) | collective-permute-done | bytes 294944 | tf_op jit(solution)/shard_map/ppermute | solution.py:47
  32.4 1.8 %collective-permute-done = bf16[128,1152]{1,0:T(8,128)(2,1)S(1)} collective-permute-done((bf16[128,1152]{1,0:T(8,128)(2,1)S(1)}, bf16[128,1152]{1,0:T(8,128)(2,1)S(1)}, u32[]{:S(2)}, u32[]{:S(2)}) %collective-permute-start) | collective-permute-done | bytes 294944 | tf_op jit(solution)/shard_map/ppermute | solution.py:48
  34.2 0.4 fusion.6
  34.6 0.2 convolution_convert_fusion.2
  34.9 1.9 %collective-permute-start.4 = (bf16[128,1152]{1,0:T(8,128)(2,1)S(1)}, bf16[128,1152]{1,0:T(8,128)(2,1)S(1)}, u32[]{:S(2)}, u32[]{:S(2)}) collective-permute-start(bf16[128,1152]{1,0:T(8,128)(2,1)S(1)} %convolution_convert_fusion.2), channel_id=1, source_target_pairs={{0,2},{2,4},{4,6},{6,8},{8,10},{10,12},{12,14},{14,16},{16,18},{18... | collective-permute-start | bytes 884744 | tf_op jit(solution)/shard_map/ppermute | solution.py:47
  36.8 0.4 convolution_convert_fusion.1
  37.2 2.2 %collective-permute-start.3 = (bf16[128,1152]{1,0:T(8,128)(2,1)S(1)}, bf16[128,1152]{1,0:T(8,128)(2,1)S(1)}, u32[]{:S(2)}, u32[]{:S(2)}) collective-permute-start(bf16[128,1152]{1,0:T(8,128)(2,1)S(1)} %convolution_convert_fusion.1), channel_id=1, source_target_pairs={{0,1},{1,0},{2,3},{3,2},{4,5},{5,4},{6,7},{7,6},{8,9},{9,8},{10,11... | collective-permute-start | bytes 884744 | tf_op jit(solution)/shard_map/ppermute | solution.py:49
  39.4 0.2 convolution_convert_fusion
  39.6 7.0 %collective-permute-start.5 = (bf16[128,1152]{1,0:T(8,128)(2,1)S(1)}, bf16[128,1152]{1,0:T(8,128)(2,1)S(1)}, u32[]{:S(2)}, u32[]{:S(2)}) collective-permute-start(bf16[128,1152]{1,0:T(8,128)(2,1)S(1)} %convolution_convert_fusion), channel_id=1, source_target_pairs={{2,0},{4,2},{6,4},{8,6},{10,8},{12,10},{14,12},{16,14},{18,16},{20... | collective-permute-start | bytes 884744 | tf_op jit(solution)/shard_map/ppermute | solution.py:48
  46.6 0.0 collective-permute-done.4
  46.7 0.3 convolution_add_fusion
  46.9 7.8 %collective-permute-done.3 = bf16[128,1152]{1,0:T(8,128)(2,1)S(1)} collective-permute-done((bf16[128,1152]{1,0:T(8,128)(2,1)S(1)}, bf16[128,1152]{1,0:T(8,128)(2,1)S(1)}, u32[]{:S(2)}, u32[]{:S(2)}) %collective-permute-start.3) | collective-permute-done | bytes 294944 | tf_op jit(solution)/shard_map/ppermute | solution.py:49
  54.7 0.5 multiply_reduce_fusion.1
  55.2 1.0 %subtract_multiply_fusion.1 = f32[128,1152]{1,0:T(8,128)} fusion(f32[128,1152]{1,0:T(8,128)S(1)} %copy-done.1, f32[128,1152]{1,0:T(8,128)S(1)} %get-tuple-element.23, bf16[128,1152]{1,0:T(8,128)(2,1)S(1)} %collective-permute-done.3, f32[128]{0:T(128)S(1)} %get-tuple-element.22, f32[128]{0:T(128)S(1)} %add_rsqrt_fusion.1), kind=kLoop, calls=%fused_computation.29 | loop fusion | flops 884736 | bytes 2065408 | tf_op jit(solution)/shard_map/mul | solution.py:25
  56.2 0.0 collective-permute-done.5
  56.2 0.2 multiply_reduce_fusion
  56.4 1.0 %subtract_multiply_fusion = f32[128,1152]{1,0:T(8,128)} fusion(f32[128,1152]{1,0:T(8,128)S(1)} %copy-done, f32[128,1152]{1,0:T(8,128)S(1)} %convolution_add_fusion, bf16[128,1152]{1,0:T(8,128)(2,1)S(1)} %collective-permute-done.5, f32[128]{0:T(128)S(1)} %multiply_reduce_fusion, f32[128]{0:T(128)S(1)} %add_rsqrt_fusion), kind=kLoop, calls=%fused_computation.26 | loop fusion | flops 884736 | bytes 2065408 | tf_op jit(solution)/shard_map/mul | solution.py:25
  (5 shorter events, 0.0 us)
Async XLA Ops:
  0.6 1.3 %copy-start.1 = (f32[128,1152]{1,0:T(8,128)S(1)}, f32[128,1152]{1,0:T(8,128)}, u32[]{:S(2)}) copy-start(f32[128,1152]{1,0:T(8,128)} %param.5) | copy-start | bytes 1769476
  1.9 8.5 %copy-start = (f32[128,1152]{1,0:T(8,128)S(1)}, f32[128,1152]{1,0:T(8,128)}, u32[]{:S(2)}) copy-start(f32[128,1152]{1,0:T(8,128)} %param.4) | copy-start | bytes 1769476
  2.0 29.3 %collective-permute-start.2 = (bf16[128,1152]{1,0:T(8,128)(2,1)S(1)}, bf16[128,1152]{1,0:T(8,128)(2,1)S(1)}, u32[]{:S(2)}, u32[]{:S(2)}) collective-permute-start(bf16[128,1152]{1,0:T(8,128)(2,1)S(1)} %multiply_convert_fusion.1), channel_id=1, source_target_pairs={{0,1},{1,0},{2,3},{3,2},{4,5},{5,4},{6,7},{7,6},{8,9},{9,8},{10,11... | collective-permute-start | bytes 884744 | tf_op jit(solution)/shard_map/ppermute | solution.py:49
  10.6 21.8 %collective-permute-start.1 = (bf16[128,1152]{1,0:T(8,128)(2,1)S(1)}, bf16[128,1152]{1,0:T(8,128)(2,1)S(1)}, u32[]{:S(2)}, u32[]{:S(2)}) collective-permute-start(bf16[128,1152]{1,0:T(8,128)(2,1)S(1)} %multiply_convert_fusion), channel_id=1, source_target_pairs={{0,2},{2,4},{4,6},{6,8},{8,10},{10,12},{12,14},{14,16},{16,18},{18... | collective-permute-start | bytes 884744 | tf_op jit(solution)/shard_map/ppermute | solution.py:47
  12.5 21.7 %collective-permute-start = (bf16[128,1152]{1,0:T(8,128)(2,1)S(1)}, bf16[128,1152]{1,0:T(8,128)(2,1)S(1)}, u32[]{:S(2)}, u32[]{:S(2)}) collective-permute-start(bf16[128,1152]{1,0:T(8,128)(2,1)S(1)} %multiply_convert_fusion), channel_id=1, source_target_pairs={{2,0},{4,2},{6,4},{8,6},{10,8},{12,10},{14,12},{16,14},{18,16},{20... | collective-permute-start | bytes 884744 | tf_op jit(solution)/shard_map/ppermute | solution.py:48
  34.9 11.8 %collective-permute-start.4 = (bf16[128,1152]{1,0:T(8,128)(2,1)S(1)}, bf16[128,1152]{1,0:T(8,128)(2,1)S(1)}, u32[]{:S(2)}, u32[]{:S(2)}) collective-permute-start(bf16[128,1152]{1,0:T(8,128)(2,1)S(1)} %convolution_convert_fusion.2), channel_id=1, source_target_pairs={{0,2},{2,4},{4,6},{6,8},{8,10},{10,12},{12,14},{14,16},{16,18},{18... | collective-permute-start | bytes 884744 | tf_op jit(solution)/shard_map/ppermute | solution.py:47
  37.2 17.5 %collective-permute-start.3 = (bf16[128,1152]{1,0:T(8,128)(2,1)S(1)}, bf16[128,1152]{1,0:T(8,128)(2,1)S(1)}, u32[]{:S(2)}, u32[]{:S(2)}) collective-permute-start(bf16[128,1152]{1,0:T(8,128)(2,1)S(1)} %convolution_convert_fusion.1), channel_id=1, source_target_pairs={{0,1},{1,0},{2,3},{3,2},{4,5},{5,4},{6,7},{7,6},{8,9},{9,8},{10,11... | collective-permute-start | bytes 884744 | tf_op jit(solution)/shard_map/ppermute | solution.py:49
  39.6 16.5 %collective-permute-start.5 = (bf16[128,1152]{1,0:T(8,128)(2,1)S(1)}, bf16[128,1152]{1,0:T(8,128)(2,1)S(1)}, u32[]{:S(2)}, u32[]{:S(2)}) collective-permute-start(bf16[128,1152]{1,0:T(8,128)(2,1)S(1)} %convolution_convert_fusion), channel_id=1, source_target_pairs={{2,0},{4,2},{6,4},{8,6},{10,8},{12,10},{14,12},{16,14},{18,16},{20... | collective-permute-start | bytes 884744 | tf_op jit(solution)/shard_map/ppermute | solution.py:48

commit v4 on v2

--- a/solution.py
+++ b/solution.py
@@ -43,17 +43,17 @@
     chain = [group * halves + half for half in range(halves) for group in range(groups)]
     onward = [(chain[i], chain[(i + 1) % len(chain)]) for i in range(len(chain))]
     back = [(target, source) for source, target in onward]
-    swap = [(0, 1), (1, 0)]
-    to_right = lambda block: lax.ppermute(block, ("dp", "sub"), onward)
-    to_left = lambda block: lax.ppermute(block, ("dp", "sub"), back)
-    across = lambda block: lax.ppermute(block, "sub", swap)
+    swap = [(group * halves + half, group * halves + 1 - half) for group in range(groups) for half in range(halves)]
+    late = [pair for pair in swap if pair[0] // halves % 16 == 15]
+    early = [pair for pair in swap if pair[0] // halves % 16 != 15]
+    send = lambda block, pairs: lax.ppermute(block, ("dp", "sub"), pairs)
     rows = picture_encoder_embeds.shape[0]
     after = lambda value, earlier: lax.optimization_barrier((value, earlier))[0]
 
     text, text_inverse = normalize(caption_encoder_embeds)
-    far_text = across(text)
+    far_text = send(text, swap)
     image, image_inverse = normalize(after(picture_encoder_embeds, text))
-    left_image, right_image = to_right(image), to_left(image)
+    right_image, left_image = send(image, back), send(image, onward)
     texts = jnp.concatenate([text, far_text])
     own = band_coeffs(score_multiplier, score_offset_term, image, texts, rows)
     left_image, right_image, own = lax.optimization_barrier((left_image, right_image, own))
@@ -61,17 +61,23 @@
     side_coeffs = band_coeffs(score_multiplier, score_offset_term, sides, texts, 0)
     images = jnp.concatenate([image, sides])
     coeffs = jnp.concatenate([own, side_coeffs])
+    place = lax.axis_index("dp") % 16
     far_dir = transposed_times(coeffs[:, rows:], images).astype(BF16)
-    coeffs, far_dir = lax.optimization_barrier((coeffs, far_dir))
-    far_dir = across(far_dir)
-    right_dir = times(coeffs[2 * rows :], texts).astype(BF16)
-    from_left = to_right(right_dir)
-    left_dir = times(coeffs[rows : 2 * rows], texts).astype(BF16)
-    from_right = to_left(left_dir)
-    text_dir = transposed_times(coeffs[:, :rows], images) + far_dir.astype(F32)
+    right_dir = times(after(coeffs[2 * rows :], far_dir), texts).astype(BF16)
+    early_dir = send(far_dir, early)
+    from_left = send(right_dir, onward)
+    left_dir = times(after(coeffs[rows : 2 * rows], right_dir), texts).astype(BF16)
+    from_right = send(left_dir, back)
+    late_block = jnp.where(place == 15, after(far_dir, left_dir), jnp.zeros_like(far_dir))
+    late_dir = send(late_block, late)
+    text_part = transposed_times(coeffs[:, :rows], images) + early_dir.astype(F32)
+    from_left, text_part = lax.optimization_barrier((from_left, text_part))
+    image_part = times(coeffs[:rows], texts) + from_left.astype(F32)
+    late_dir, image_part = lax.optimization_barrier((late_dir, image_part))
+    text_dir = text_part + late_dir.astype(F32)
     text_grad = backward_norm(caption_encoder_embeds, text_inverse, text_dir)
-    from_left, from_right, text_grad = lax.optimization_barrier((from_left, from_right, text_grad))
-    image_dir = times(coeffs[:rows], texts) + from_left.astype(F32) + from_right.astype(F32)
+    from_right, text_grad = lax.optimization_barrier((from_right, text_grad))
+    image_dir = image_part + from_right.astype(F32)
     image_grad = backward_norm(picture_encoder_embeds, image_inverse, image_dir)
     return (image_grad, text_grad)
 

time: 64.1 us -> 56.8 us (0.89)
  waiting for transfers between devices: 13.1 us -> 5.56 us
    ppermute x6 -> x7, waiting for transfers between devices: 13.1 us -> 5.56 us  [shards(): send = lambda block, pairs: lax.ppermute(block, ('dp', 'sub'), pairs)]
    ppermute x6 -> x7, starting transfers between devices: 42.5 us -> 42.5 us  [shards(): send = lambda block, pairs: lax.ppermute(block, ('dp', 'sub'), pairs)]
  transfers between devices with their start and end apart: 6 -> 7, of which waited for: 4 -> 3; matrix products, arithmetic and copies ran while one was open for 4% -> 5% of each run, Pallas kernels for 0% -> 0%
where the time goes in v4:
time: 56.8 us; the launch traced here: 56.5 us
  starting transfers between devices  42.5 us (75%)
  waiting for transfers between devices  5.56 us (10%)
  other arithmetic  4.03 us (7%)
  matrix products  2.25 us (4%)
  between operations  2.14 us (4%)
    ppermute x7, starting transfers between devices, shards(): send = lambda block, pairs: lax.ppermute(block, ('dp', 'sub'), pairs)  42.5 us
    ppermute x7, waiting for transfers between devices, shards(): send = lambda block, pairs: lax.ppermute(block, ('dp', 'sub'), pairs)  5.56 us
    mul x2, other arithmetic, backward_norm(): (direction - unit * jnp.sum(unit * direction, axis=-1, keepdims=True)) *...  1.98 us
    reduce_sum x2, other arithmetic, normalize(): jnp.sum(values * values, axis=-1, keepdims=True) + 1e-06  1.37 us
  transfers between devices with their start and end apart: 7, of which 3 were waited for; matrix products, arithmetic and copies ran while one was open for 5% of the time, Pallas kernels for 0%

profile of v4, /device:TPU:64, one launch (start us, length us, event | category | flops | bytes accessed | tf_op | source)
XLA Modules:
  0.0 56.5 jit_solution(138815610977694828)
XLA Ops:
  0.6 0.0 copy-start
  0.6 1.2 %multiply_reduce_fusion.3 = f32[128]{0:T(128)S(1)} fusion(f32[128,1152]{1,0:T(8,128)} %param.5), kind=kLoop, calls=%fused_computation.35 | loop fusion | flops 294784 | bytes 590336 | tf_op jit(solution)/shard_map/reduce_sum | solution.py:19
  1.9 0.0 copy-start.1
  1.9 0.0 copy-done
  1.9 0.1 multiply_convert_fusion.1
  2.0 14.3 %collective-permute-start.2 = (bf16[128,1152]{1,0:T(8,128)(2,1)S(1)}, bf16[128,1152]{1,0:T(8,128)(2,1)S(1)}, u32[]{:S(2)}, u32[]{:S(2)}) collective-permute-start(bf16[128,1152]{1,0:T(8,128)(2,1)S(1)} %multiply_convert_fusion.1), channel_id=1, source_target_pairs={{0,1},{1,0},{2,3},{3,2},{4,5},{5,4},{6,7},{7,6},{8,9},{9,8},{10,11... | collective-permute-start | bytes 884744 | tf_op jit(solution)/shard_map/ppermute | solution.py:49
  16.4 0.0 copy-done.1
  16.4 0.1 multiply_reduce_fusion.2
  16.5 0.1 multiply_convert_fusion
  16.6 1.9 %collective-permute-start = (bf16[128,1152]{1,0:T(8,128)(2,1)S(1)}, bf16[128,1152]{1,0:T(8,128)(2,1)S(1)}, u32[]{:S(2)}, u32[]{:S(2)}) collective-permute-start(bf16[128,1152]{1,0:T(8,128)(2,1)S(1)} %multiply_convert_fusion), channel_id=1, source_target_pairs={{0,2},{2,4},{4,6},{6,8},{8,10},{10,12},{12,14},{14,16},{16,18},{18... | collective-permute-start | bytes 884744 | tf_op jit(solution)/shard_map/ppermute | solution.py:49
  18.6 9.9 %collective-permute-start.1 = (bf16[128,1152]{1,0:T(8,128)(2,1)S(1)}, bf16[128,1152]{1,0:T(8,128)(2,1)S(1)}, u32[]{:S(2)}, u32[]{:S(2)}) collective-permute-start(bf16[128,1152]{1,0:T(8,128)(2,1)S(1)} %multiply_convert_fusion), channel_id=1, source_target_pairs={{2,0},{4,2},{6,4},{8,6},{10,8},{12,10},{14,12},{16,14},{18,16},{20... | collective-permute-start | bytes 884744 | tf_op jit(solution)/shard_map/ppermute | solution.py:49
  29.8 0.0 collective-permute-done.2
  29.8 0.4 fusion.14
  30.1 2.6 %collective-permute-done = bf16[128,1152]{1,0:T(8,128)(2,1)S(1)} collective-permute-done((bf16[128,1152]{1,0:T(8,128)(2,1)S(1)}, bf16[128,1152]{1,0:T(8,128)(2,1)S(1)}, u32[]{:S(2)}, u32[]{:S(2)}) %collective-permute-start) | collective-permute-done | bytes 294944 | tf_op jit(solution)/shard_map/ppermute | solution.py:49
  32.7 0.5 collective-permute-done.1
  33.2 0.4 fusion.6
  33.6 0.4 convolution_convert_fusion.2
  34.0 4.7 %collective-permute-start.5 = (bf16[128,1152]{1,0:T(8,128)(2,1)S(1)}, bf16[128,1152]{1,0:T(8,128)(2,1)S(1)}, u32[]{:S(2)}, u32[]{:S(2)}) collective-permute-start(bf16[128,1152]{1,0:T(8,128)(2,1)S(1)} %convolution_convert_fusion.2), channel_id=1, source_target_pairs={{0,1},{1,0},{2,3},{3,2},{4,5},{5,4},{6,7},{7,6},{8,9},{9,8},{10,11... | collective-permute-start | bytes 884744 | tf_op jit(solution)/shard_map/ppermute | solution.py:49
  38.7 0.2 convolution_convert_fusion.1
  39.0 1.9 %collective-permute-start.4 = (bf16[128,1152]{1,0:T(8,128)(2,1)S(1)}, bf16[128,1152]{1,0:T(8,128)(2,1)S(1)}, u32[]{:S(2)}, u32[]{:S(2)}) collective-permute-start(bf16[128,1152]{1,0:T(8,128)(2,1)S(1)} %convolution_convert_fusion.1), channel_id=1, source_target_pairs={{0,2},{2,4},{4,6},{6,8},{8,10},{10,12},{12,14},{14,16},{16,18},{18... | collective-permute-start | bytes 884744 | tf_op jit(solution)/shard_map/ppermute | solution.py:49
  40.9 0.2 convolution_convert_fusion
  41.1 9.1 %collective-permute-start.6 = (bf16[128,1152]{1,0:T(8,128)(2,1)S(1)}, bf16[128,1152]{1,0:T(8,128)(2,1)S(1)}, u32[]{:S(2)}, u32[]{:S(2)}) collective-permute-start(bf16[128,1152]{1,0:T(8,128)(2,1)S(1)} %convolution_convert_fusion), channel_id=1, source_target_pairs={{2,0},{4,2},{6,4},{8,6},{10,8},{12,10},{14,12},{16,14},{18,16},{20... | collective-permute-start | bytes 884744 | tf_op jit(solution)/shard_map/ppermute | solution.py:49
  50.3 0.7 %collective-permute-start.3 = (bf16[128,1152]{1,0:T(8,128)(2,1)S(1)}, bf16[128,1152]{1,0:T(8,128)(2,1)S(1)}, u32[]{:S(2)}, u32[]{:S(2)}) collective-permute-start(bf16[128,1152]{1,0:T(8,128)(2,1)S(1)} %broadcast_select_fusion), channel_id=1, source_target_pairs={{30,31},{31,30},{62,63},{63,62},{94,95},{95,94},{126,127},{127,126... | collective-permute-start | bytes 884744 | tf_op jit(solution)/shard_map/ppermute | solution.py:49
  50.9 0.0 collective-permute-done.5
  51.0 0.4 convert_add_fusion.2
  51.3 2.5 %collective-permute-done.4 = bf16[128,1152]{1,0:T(8,128)(2,1)S(1)} collective-permute-done((bf16[128,1152]{1,0:T(8,128)(2,1)S(1)}, bf16[128,1152]{1,0:T(8,128)(2,1)S(1)}, u32[]{:S(2)}, u32[]{:S(2)}) %collective-permute-start.4) | collective-permute-done | bytes 294944 | tf_op jit(solution)/shard_map/ppermute | solution.py:49
  53.8 0.3 convolution_add_fusion
  54.1 0.0 collective-permute-done.3
  54.1 0.2 multiply_reduce_fusion.1
  54.3 1.0 %subtract_multiply_fusion.1 = f32[128,1152]{1,0:T(8,128)} fusion(f32[128,1152]{1,0:T(8,128)S(1)} %copy-done, f32[128,1152]{1,0:T(8,128)S(1)} %convert_add_fusion.2, bf16[128,1152]{1,0:T(8,128)(2,1)S(1)} %collective-permute-done.3, f32[128]{0:T(128)S(1)} %multiply_reduce_fusion.1, f32[128]{0:T(128)S(1)} %add_rsqrt_fusion.1), kind=kLoop, calls=%fused_computation.29 | loop fusion | flops 884736 | bytes 2065408 | tf_op jit(solution)/shard_map/mul | solution.py:25
  55.3 0.0 collective-permute-done.6
  55.3 0.2 multiply_reduce_fusion
  55.5 1.0 %subtract_multiply_fusion = f32[128,1152]{1,0:T(8,128)} fusion(f32[128,1152]{1,0:T(8,128)S(1)} %copy-done.1, f32[128,1152]{1,0:T(8,128)S(1)} %convolution_add_fusion, bf16[128,1152]{1,0:T(8,128)(2,1)S(1)} %collective-permute-done.6, f32[128]{0:T(128)S(1)} %multiply_reduce_fusion, f32[128]{0:T(128)S(1)} %add_rsqrt_fusion), kind=kLoop, calls=%fused_computation.26 | loop fusion | flops 884736 | bytes 2065408 | tf_op jit(solution)/shard_map/mul | solution.py:25
  (5 shorter events, 0.1 us)
Async XLA Ops:
  0.6 1.3 %copy-start = (f32[128,1152]{1,0:T(8,128)S(1)}, f32[128,1152]{1,0:T(8,128)}, u32[]{:S(2)}) copy-start(f32[128,1152]{1,0:T(8,128)} %param.5) | copy-start | bytes 1769476
  1.9 14.5 %copy-start.1 = (f32[128,1152]{1,0:T(8,128)S(1)}, f32[128,1152]{1,0:T(8,128)}, u32[]{:S(2)}) copy-start(f32[128,1152]{1,0:T(8,128)} %param.4) | copy-start | bytes 1769476
  2.0 27.7 %collective-permute-start.2 = (bf16[128,1152]{1,0:T(8,128)(2,1)S(1)}, bf16[128,1152]{1,0:T(8,128)(2,1)S(1)}, u32[]{:S(2)}, u32[]{:S(2)}) collective-permute-start(bf16[128,1152]{1,0:T(8,128)(2,1)S(1)} %multiply_convert_fusion.1), channel_id=1, source_target_pairs={{0,1},{1,0},{2,3},{3,2},{4,5},{5,4},{6,7},{7,6},{8,9},{9,8},{10,11... | collective-permute-start | bytes 884744 | tf_op jit(solution)/shard_map/ppermute | solution.py:49
  16.6 16.1 %collective-permute-start = (bf16[128,1152]{1,0:T(8,128)(2,1)S(1)}, bf16[128,1152]{1,0:T(8,128)(2,1)S(1)}, u32[]{:S(2)}, u32[]{:S(2)}) collective-permute-start(bf16[128,1152]{1,0:T(8,128)(2,1)S(1)} %multiply_convert_fusion), channel_id=1, source_target_pairs={{0,2},{2,4},{4,6},{6,8},{8,10},{10,12},{12,14},{14,16},{16,18},{18... | collective-permute-start | bytes 884744 | tf_op jit(solution)/shard_map/ppermute | solution.py:49
  18.6 14.6 %collective-permute-start.1 = (bf16[128,1152]{1,0:T(8,128)(2,1)S(1)}, bf16[128,1152]{1,0:T(8,128)(2,1)S(1)}, u32[]{:S(2)}, u32[]{:S(2)}) collective-permute-start(bf16[128,1152]{1,0:T(8,128)(2,1)S(1)} %multiply_convert_fusion), channel_id=1, source_target_pairs={{2,0},{4,2},{6,4},{8,6},{10,8},{12,10},{14,12},{16,14},{18,16},{20... | collective-permute-start | bytes 884744 | tf_op jit(solution)/shard_map/ppermute | solution.py:49
  34.0 17.0 %collective-permute-start.5 = (bf16[128,1152]{1,0:T(8,128)(2,1)S(1)}, bf16[128,1152]{1,0:T(8,128)(2,1)S(1)}, u32[]{:S(2)}, u32[]{:S(2)}) collective-permute-start(bf16[128,1152]{1,0:T(8,128)(2,1)S(1)} %convolution_convert_fusion.2), channel_id=1, source_target_pairs={{0,1},{1,0},{2,3},{3,2},{4,5},{5,4},{6,7},{7,6},{8,9},{9,8},{10,11... | collective-permute-start | bytes 884744 | tf_op jit(solution)/shard_map/ppermute | solution.py:49
  39.0 14.9 %collective-permute-start.4 = (bf16[128,1152]{1,0:T(8,128)(2,1)S(1)}, bf16[128,1152]{1,0:T(8,128)(2,1)S(1)}, u32[]{:S(2)}, u32[]{:S(2)}) collective-permute-start(bf16[128,1152]{1,0:T(8,128)(2,1)S(1)} %convolution_convert_fusion.1), channel_id=1, source_target_pairs={{0,2},{2,4},{4,6},{6,8},{8,10},{10,12},{12,14},{14,16},{16,18},{18... | collective-permute-start | bytes 884744 | tf_op jit(solution)/shard_map/ppermute | solution.py:49
  41.1 14.2 %collective-permute-start.6 = (bf16[128,1152]{1,0:T(8,128)(2,1)S(1)}, bf16[128,1152]{1,0:T(8,128)(2,1)S(1)}, u32[]{:S(2)}, u32[]{:S(2)}) collective-permute-start(bf16[128,1152]{1,0:T(8,128)(2,1)S(1)} %convolution_convert_fusion), channel_id=1, source_target_pairs={{2,0},{4,2},{6,4},{8,6},{10,8},{12,10},{14,12},{16,14},{18,16},{20... | collective-permute-start | bytes 884744 | tf_op jit(solution)/shard_map/ppermute | solution.py:49
  50.3 3.8 %collective-permute-start.3 = (bf16[128,1152]{1,0:T(8,128)(2,1)S(1)}, bf16[128,1152]{1,0:T(8,128)(2,1)S(1)}, u32[]{:S(2)}, u32[]{:S(2)}) collective-permute-start(bf16[128,1152]{1,0:T(8,128)(2,1)S(1)} %broadcast_select_fusion), channel_id=1, source_target_pairs={{30,31},{31,30},{62,63},{63,62},{94,95},{95,94},{126,127},{127,126... | collective-permute-start | bytes 884744 | tf_op jit(solution)/shard_map/ppermute | solution.py:49

commit v5 on v4

--- a/solution.py
+++ b/solution.py
@@ -46,6 +46,7 @@
     swap = [(group * halves + half, group * halves + 1 - half) for group in range(groups) for half in range(halves)]
     late = [pair for pair in swap if pair[0] // halves % 16 == 15]
     early = [pair for pair in swap if pair[0] // halves % 16 != 15]
+    wraps, inner = onward[127::128], [pair for i, pair in enumerate(onward) if i % 128 != 127]
     send = lambda block, pairs: lax.ppermute(block, ("dp", "sub"), pairs)
     rows = picture_encoder_embeds.shape[0]
     after = lambda value, earlier: lax.optimization_barrier((value, earlier))[0]
@@ -62,23 +63,25 @@
     images = jnp.concatenate([image, sides])
     coeffs = jnp.concatenate([own, side_coeffs])
     place = lax.axis_index("dp") % 16
-    far_dir = transposed_times(coeffs[:, rows:], images).astype(BF16)
-    right_dir = times(after(coeffs[2 * rows :], far_dir), texts).astype(BF16)
+    right_dir = times(coeffs[2 * rows :], texts).astype(BF16)
+    far_dir = transposed_times(after(coeffs[:, rows:], right_dir), images).astype(BF16)
+    from_wrap = send(right_dir, wraps)
     early_dir = send(far_dir, early)
-    from_left = send(right_dir, onward)
+    right_dir = jnp.where(place < 16, after(right_dir, far_dir), jnp.zeros_like(right_dir))
+    from_left = send(right_dir, inner)
     left_dir = times(after(coeffs[rows : 2 * rows], right_dir), texts).astype(BF16)
     from_right = send(left_dir, back)
     late_block = jnp.where(place == 15, after(far_dir, left_dir), jnp.zeros_like(far_dir))
     late_dir = send(late_block, late)
+    image_part = times(coeffs[:rows], texts) + from_wrap.astype(F32) + from_left.astype(F32)
+    from_right, image_part = lax.optimization_barrier((from_right, image_part))
+    image_dir = image_part + from_right.astype(F32)
+    image_grad = backward_norm(picture_encoder_embeds, image_inverse, image_dir)
+    early_dir, image_grad = lax.optimization_barrier((early_dir, image_grad))
     text_part = transposed_times(coeffs[:, :rows], images) + early_dir.astype(F32)
-    from_left, text_part = lax.optimization_barrier((from_left, text_part))
-    image_part = times(coeffs[:rows], texts) + from_left.astype(F32)
-    late_dir, image_part = lax.optimization_barrier((late_dir, image_part))
+    late_dir, text_part = lax.optimization_barrier((late_dir, text_part))
     text_dir = text_part + late_dir.astype(F32)
     text_grad = backward_norm(caption_encoder_embeds, text_inverse, text_dir)
-    from_right, text_grad = lax.optimization_barrier((from_right, text_grad))
-    image_dir = image_part + from_right.astype(F32)
-    image_grad = backward_norm(picture_encoder_embeds, image_inverse, image_dir)
     return (image_grad, text_grad)
 
 

time: 56.8 us -> 56.7 us (level)
  the two profiles are of different devices: /device:TPU:64 before, /device:TPU:30 now
where the time goes in v5:
time: 56.7 us; the launch traced here: 56.3 us
  starting transfers between devices  38.3 us (68%)
  waiting for transfers between devices  9.17 us (16%)
  other arithmetic  4.07 us (7%)
  matrix products  2.23 us (4%)
  between operations  2.18 us (4%)
    ppermute x8, starting transfers between devices, shards(): send = lambda block, pairs: lax.ppermute(block, ('dp', 'sub'), pairs)  38.3 us
    ppermute x8, waiting for transfers between devices, shards(): send = lambda block, pairs: lax.ppermute(block, ('dp', 'sub'), pairs)  9.17 us
    mul x2, other arithmetic, backward_norm(): (direction - unit * jnp.sum(unit * direction, axis=-1, keepdims=True)) *...  1.98 us
    reduce_sum x2, other arithmetic, normalize(): jnp.sum(values * values, axis=-1, keepdims=True) + 1e-06  1.37 us
  transfers between devices with their start and end apart: 8, of which 5 were waited for; matrix products, arithmetic and copies ran while one was open for 5% of the time, Pallas kernels for 0%

profile of v5, /device:TPU:30, one launch (start us, length us, event | category | flops | bytes accessed | tf_op | source)
XLA Modules:
  0.0 56.3 jit_solution(12667947866381175695)
XLA Ops:
  0.6 0.0 copy-start.1
  0.6 1.2 %multiply_reduce_fusion.3 = f32[128]{0:T(128)S(1)} fusion(f32[128,1152]{1,0:T(8,128)} %param.5), kind=kLoop, calls=%fused_computation.36 | loop fusion | flops 294784 | bytes 590336 | tf_op jit(solution)/shard_map/reduce_sum | solution.py:19
  1.9 0.0 copy-start
  1.9 0.0 copy-done.1
  1.9 0.1 multiply_convert_fusion.1
  2.0 7.4 %collective-permute-start.2 = (bf16[128,1152]{1,0:T(8,128)(2,1)S(1)}, bf16[128,1152]{1,0:T(8,128)(2,1)S(1)}, u32[]{:S(2)}, u32[]{:S(2)}) collective-permute-start(bf16[128,1152]{1,0:T(8,128)(2,1)S(1)} %multiply_convert_fusion.1), channel_id=1, source_target_pairs={{0,1},{1,0},{2,3},{3,2},{4,5},{5,4},{6,7},{7,6},{8,9},{9,8},{10,11... | collective-permute-start | bytes 884744 | tf_op jit(solution)/shard_map/ppermute | solution.py:50
  9.5 0.0 copy-done
  9.5 0.1 multiply_reduce_fusion.2
  9.6 0.1 multiply_convert_fusion
  9.7 1.9 %collective-permute-start = (bf16[128,1152]{1,0:T(8,128)(2,1)S(1)}, bf16[128,1152]{1,0:T(8,128)(2,1)S(1)}, u32[]{:S(2)}, u32[]{:S(2)}) collective-permute-start(bf16[128,1152]{1,0:T(8,128)(2,1)S(1)} %multiply_convert_fusion), channel_id=1, source_target_pairs={{0,2},{2,4},{4,6},{6,8},{8,10},{10,12},{12,14},{14,16},{16,18},{18... | collective-permute-start | bytes 884744 | tf_op jit(solution)/shard_map/ppermute | solution.py:50
  11.6 17.4 %collective-permute-start.1 = (bf16[128,1152]{1,0:T(8,128)(2,1)S(1)}, bf16[128,1152]{1,0:T(8,128)(2,1)S(1)}, u32[]{:S(2)}, u32[]{:S(2)}) collective-permute-start(bf16[128,1152]{1,0:T(8,128)(2,1)S(1)} %multiply_convert_fusion), channel_id=1, source_target_pairs={{2,0},{4,2},{6,4},{8,6},{10,8},{12,10},{14,12},{16,14},{18,16},{20... | collective-permute-start | bytes 884744 | tf_op jit(solution)/shard_map/ppermute | solution.py:50
  30.4 0.0 collective-permute-done.2
  30.4 0.4 fusion.15
  30.7 0.8 %collective-permute-done = bf16[128,1152]{1,0:T(8,128)(2,1)S(1)} collective-permute-done((bf16[128,1152]{1,0:T(8,128)(2,1)S(1)}, bf16[128,1152]{1,0:T(8,128)(2,1)S(1)}, u32[]{:S(2)}, u32[]{:S(2)}) %collective-permute-start) | collective-permute-done | bytes 294944 | tf_op jit(solution)/shard_map/ppermute | solution.py:50
  31.5 1.8 %collective-permute-done.1 = bf16[128,1152]{1,0:T(8,128)(2,1)S(1)} collective-permute-done((bf16[128,1152]{1,0:T(8,128)(2,1)S(1)}, bf16[128,1152]{1,0:T(8,128)(2,1)S(1)}, u32[]{:S(2)}, u32[]{:S(2)}) %collective-permute-start.1) | collective-permute-done | bytes 294944 | tf_op jit(solution)/shard_map/ppermute | solution.py:50
  33.3 0.4 fusion.7
  33.7 0.0 copy-start.2
  33.7 0.2 convolution_convert_fusion.2
  33.9 0.4 copy-done.2
  34.3 0.7 %collective-permute-start.5 = (bf16[128,1152]{1,0:T(8,128)(2,1)S(1)}, bf16[128,1152]{1,0:T(8,128)(2,1)S(1)}, u32[]{:S(2)}, u32[]{:S(2)}) collective-permute-start(bf16[128,1152]{1,0:T(8,128)(2,1)S(1)} %convolution_convert_fusion.2), channel_id=1, source_target_pairs={{254,256},{510,512},{766,768},{1022,1},{255,257},{511,513},{767,76... | collective-permute-start | bytes 884744 | tf_op jit(solution)/shard_map/ppermute | solution.py:50
  35.0 0.4 convolution_convert_fusion.1
  35.4 0.0 slice-start
  35.4 2.5 %collective-permute-start.3 = (bf16[128,1152]{1,0:T(8,128)(2,1)S(1)}, bf16[128,1152]{1,0:T(8,128)(2,1)S(1)}, u32[]{:S(2)}, u32[]{:S(2)}) collective-permute-start(bf16[128,1152]{1,0:T(8,128)(2,1)S(1)} %convolution_convert_fusion.1), channel_id=1, source_target_pairs={{0,1},{1,0},{2,3},{3,2},{4,5},{5,4},{6,7},{7,6},{8,9},{9,8},{10,11... | collective-permute-start | bytes 884744 | tf_op jit(solution)/shard_map/ppermute | solution.py:50
  38.0 1.9 %collective-permute-start.6 = (bf16[128,1152]{1,0:T(8,128)(2,1)S(1)}, bf16[128,1152]{1,0:T(8,128)(2,1)S(1)}, u32[]{:S(2)}, u32[]{:S(2)}) collective-permute-start(bf16[128,1152]{1,0:T(8,128)(2,1)S(1)} %broadcast_select_fusion.1), channel_id=1, source_target_pairs={{0,2},{2,4},{4,6},{6,8},{8,10},{10,12},{12,14},{14,16},{16,18},{18... | collective-permute-start | bytes 884744 | tf_op jit(solution)/shard_map/ppermute | solution.py:50
  39.9 0.0 slice-done
  39.9 0.2 convolution_convert_fusion
  40.2 5.8 %collective-permute-start.4 = (bf16[128,1152]{1,0:T(8,128)(2,1)S(1)}, bf16[128,1152]{1,0:T(8,128)(2,1)S(1)}, u32[]{:S(2)}, u32[]{:S(2)}) collective-permute-start(bf16[128,1152]{1,0:T(8,128)(2,1)S(1)} %convolution_convert_fusion), channel_id=1, source_target_pairs={{2,0},{4,2},{6,4},{8,6},{10,8},{12,10},{14,12},{16,14},{18,16},{20... | collective-permute-start | bytes 884744 | tf_op jit(solution)/shard_map/ppermute | solution.py:50
  46.0 0.7 %collective-permute-start.7 = (bf16[128,1152]{1,0:T(8,128)(2,1)S(1)}, bf16[128,1152]{1,0:T(8,128)(2,1)S(1)}, u32[]{:S(2)}, u32[]{:S(2)}) collective-permute-start(bf16[128,1152]{1,0:T(8,128)(2,1)S(1)} %broadcast_select_fusion), channel_id=1, source_target_pairs={{30,31},{31,30},{62,63},{63,62},{94,95},{95,94},{126,127},{127,126... | collective-permute-start | bytes 884744 | tf_op jit(solution)/shard_map/ppermute | solution.py:50
  46.6 1.5 %collective-permute-done.6 = bf16[128,1152]{1,0:T(8,128)(2,1)S(1)} collective-permute-done((bf16[128,1152]{1,0:T(8,128)(2,1)S(1)}, bf16[128,1152]{1,0:T(8,128)(2,1)S(1)}, u32[]{:S(2)}, u32[]{:S(2)}) %collective-permute-start.6) | collective-permute-done | bytes 294944 | tf_op jit(solution)/shard_map/ppermute | solution.py:50
  48.1 0.0 collective-permute-done.5
  48.1 0.3 fusion
  48.4 1.8 %collective-permute-done.4 = bf16[128,1152]{1,0:T(8,128)(2,1)S(1)} collective-permute-done((bf16[128,1152]{1,0:T(8,128)(2,1)S(1)}, bf16[128,1152]{1,0:T(8,128)(2,1)S(1)}, u32[]{:S(2)}, u32[]{:S(2)}) %collective-permute-start.4) | collective-permute-done | bytes 294944 | tf_op jit(solution)/shard_map/ppermute | solution.py:50
  50.1 0.2 multiply_reduce_fusion.1
  50.3 0.0 copy-start.3
  50.4 1.0 %subtract_multiply_fusion.1 = f32[128,1152]{1,0:T(8,128)} fusion(f32[128,1152]{1,0:T(8,128)S(1)} %copy-done, f32[128,1152]{1,0:T(8,128)S(1)} %fusion, bf16[128,1152]{1,0:T(8,128)(2,1)S(1)} %collective-permute-done.4, f32[128]{0:T(128)S(1)} %multiply_reduce_fusion.1, f32[128]{0:T(128)S(1)} %add_rsqrt_fusion), kind=kLoop, calls=%fused_computation.31 | loop fusion | flops 884736 | bytes 2065408 | tf_op jit(solution)/shard_map/mul | solution.py:25
  51.3 3.4 %collective-permute-done.3 = bf16[128,1152]{1,0:T(8,128)(2,1)S(1)} collective-permute-done((bf16[128,1152]{1,0:T(8,128)(2,1)S(1)}, bf16[128,1152]{1,0:T(8,128)(2,1)S(1)}, u32[]{:S(2)}, u32[]{:S(2)}) %collective-permute-start.3) | collective-permute-done | bytes 294944 | tf_op jit(solution)/shard_map/ppermute | solution.py:50
  54.8 0.0 copy-done.3
  54.8 0.4 convert_add_fusion.1
  55.1 0.0 collective-permute-done.7
  55.1 0.2 multiply_reduce_fusion
  55.3 1.0 %subtract_multiply_fusion = f32[128,1152]{1,0:T(8,128)} fusion(f32[128,1152]{1,0:T(8,128)S(1)} %copy-done.1, f32[128,1152]{1,0:T(8,128)S(1)} %convert_add_fusion.1, bf16[128,1152]{1,0:T(8,128)(2,1)S(1)} %collective-permute-done.7, f32[128]{0:T(128)S(1)} %multiply_reduce_fusion, f32[128]{0:T(128)S(1)} %add_rsqrt_fusion.1), kind=kLoop, calls=%fused_computation.27 | loop fusion | flops 884736 | bytes 2065408 | tf_op jit(solution)/shard_map/mul | solution.py:25
  (6 shorter events, 0.1 us)
Async XLA Ops:
  0.6 1.3 %copy-start.1 = (f32[128,1152]{1,0:T(8,128)S(1)}, f32[128,1152]{1,0:T(8,128)}, u32[]{:S(2)}) copy-start(f32[128,1152]{1,0:T(8,128)} %param.5) | copy-start | bytes 1769476
  1.9 7.6 %copy-start = (f32[128,1152]{1,0:T(8,128)S(1)}, f32[128,1152]{1,0:T(8,128)}, u32[]{:S(2)}) copy-start(f32[128,1152]{1,0:T(8,128)} %param.4) | copy-start | bytes 1769476
  2.0 28.3 %collective-permute-start.2 = (bf16[128,1152]{1,0:T(8,128)(2,1)S(1)}, bf16[128,1152]{1,0:T(8,128)(2,1)S(1)}, u32[]{:S(2)}, u32[]{:S(2)}) collective-permute-start(bf16[128,1152]{1,0:T(8,128)(2,1)S(1)} %multiply_convert_fusion.1), channel_id=1, source_target_pairs={{0,1},{1,0},{2,3},{3,2},{4,5},{5,4},{6,7},{7,6},{8,9},{9,8},{10,11... | collective-permute-start | bytes 884744 | tf_op jit(solution)/shard_map/ppermute | solution.py:50
  9.7 21.8 %collective-permute-start = (bf16[128,1152]{1,0:T(8,128)(2,1)S(1)}, bf16[128,1152]{1,0:T(8,128)(2,1)S(1)}, u32[]{:S(2)}, u32[]{:S(2)}) collective-permute-start(bf16[128,1152]{1,0:T(8,128)(2,1)S(1)} %multiply_convert_fusion), channel_id=1, source_target_pairs={{0,2},{2,4},{4,6},{6,8},{8,10},{10,12},{12,14},{14,16},{16,18},{18... | collective-permute-start | bytes 884744 | tf_op jit(solution)/shard_map/ppermute | solution.py:50
  11.6 21.6 %collective-permute-start.1 = (bf16[128,1152]{1,0:T(8,128)(2,1)S(1)}, bf16[128,1152]{1,0:T(8,128)(2,1)S(1)}, u32[]{:S(2)}, u32[]{:S(2)}) collective-permute-start(bf16[128,1152]{1,0:T(8,128)(2,1)S(1)} %multiply_convert_fusion), channel_id=1, source_target_pairs={{2,0},{4,2},{6,4},{8,6},{10,8},{12,10},{14,12},{16,14},{18,16},{20... | collective-permute-start | bytes 884744 | tf_op jit(solution)/shard_map/ppermute | solution.py:50
  33.7 0.7 %copy-start.2 = (bf16[256,256]{1,0:T(8,128)(2,1)}, bf16[256,256]{1,0:T(8,128)(2,1)S(1)}, u32[]{:S(2)}) copy-start(bf16[256,256]{1,0:T(8,128)(2,1)S(1)} %fusion.7) | copy-start | bytes 393220
  34.3 13.8 %collective-permute-start.5 = (bf16[128,1152]{1,0:T(8,128)(2,1)S(1)}, bf16[128,1152]{1,0:T(8,128)(2,1)S(1)}, u32[]{:S(2)}, u32[]{:S(2)}) collective-permute-start(bf16[128,1152]{1,0:T(8,128)(2,1)S(1)} %convolution_convert_fusion.2), channel_id=1, source_target_pairs={{254,256},{510,512},{766,768},{1022,1},{255,257},{511,513},{767,76... | collective-permute-start | bytes 884744 | tf_op jit(solution)/shard_map/ppermute | solution.py:50
  35.4 4.5 %slice-start = ((bf16[256,256]{1,0:T(8,128)(2,1)}), bf16[128,256]{1,0:T(8,128)(2,1)S(1)}, s32[]{:S(2)}) async-start(bf16[256,256]{1,0:T(8,128)(2,1)} %copy-done.2), calls=%async_computation | async-start | bytes 131072 | tf_op jit(solution)/shard_map/slice | solution.py:72
  35.4 19.4 %collective-permute-start.3 = (bf16[128,1152]{1,0:T(8,128)(2,1)S(1)}, bf16[128,1152]{1,0:T(8,128)(2,1)S(1)}, u32[]{:S(2)}, u32[]{:S(2)}) collective-permute-start(bf16[128,1152]{1,0:T(8,128)(2,1)S(1)} %convolution_convert_fusion.1), channel_id=1, source_target_pairs={{0,1},{1,0},{2,3},{3,2},{4,5},{5,4},{6,7},{7,6},{8,9},{9,8},{10,11... | collective-permute-start | bytes 884744 | tf_op jit(solution)/shard_map/ppermute | solution.py:50
  38.0 10.2 %collective-permute-start.6 = (bf16[128,1152]{1,0:T(8,128)(2,1)S(1)}, bf16[128,1152]{1,0:T(8,128)(2,1)S(1)}, u32[]{:S(2)}, u32[]{:S(2)}) collective-permute-start(bf16[128,1152]{1,0:T(8,128)(2,1)S(1)} %broadcast_select_fusion.1), channel_id=1, source_target_pairs={{0,2},{2,4},{4,6},{6,8},{8,10},{10,12},{12,14},{14,16},{16,18},{18... | collective-permute-start | bytes 884744 | tf_op jit(solution)/shard_map/ppermute | solution.py:50
  40.2 10.0 %collective-permute-start.4 = (bf16[128,1152]{1,0:T(8,128)(2,1)S(1)}, bf16[128,1152]{1,0:T(8,128)(2,1)S(1)}, u32[]{:S(2)}, u32[]{:S(2)}) collective-permute-start(bf16[128,1152]{1,0:T(8,128)(2,1)S(1)} %convolution_convert_fusion), channel_id=1, source_target_pairs={{2,0},{4,2},{6,4},{8,6},{10,8},{12,10},{14,12},{16,14},{18,16},{20... | collective-permute-start | bytes 884744 | tf_op jit(solution)/shard_map/ppermute | solution.py:50
  46.0 9.2 %collective-permute-start.7 = (bf16[128,1152]{1,0:T(8,128)(2,1)S(1)}, bf16[128,1152]{1,0:T(8,128)(2,1)S(1)}, u32[]{:S(2)}, u32[]{:S(2)}) collective-permute-start(bf16[128,1152]{1,0:T(8,128)(2,1)S(1)} %broadcast_select_fusion), channel_id=1, source_target_pairs={{30,31},{31,30},{62,63},{63,62},{94,95},{95,94},{126,127},{127,126... | collective-permute-start | bytes 884744 | tf_op jit(solution)/shard_map/ppermute | solution.py:50
  50.3 4.4 %copy-start.3 = (bf16[256,256]{1,0:T(8,128)(2,1)S(1)}, bf16[256,256]{1,0:T(8,128)(2,1)}, u32[]{:S(2)}) copy-start(bf16[256,256]{1,0:T(8,128)(2,1)} %copy-done.2) | copy-start | bytes 393220
